TPU v7x, 256 devices: a whole 4x4x8 slice. The times are simulated.
256 devices in a mesh: wide: 32 (over y_lo, z, core), blk: 8 (over y_hi, x).
Axes of the slice: x: 4, y: 4 (y_hi: 2, y_lo: 2; y = y_hi * 2 + y_lo), z: 8, core: 2. Of those that a mesh axis runs over, the one named last changes fastest.
Arguments:
- records: bfloat16 [8, 2304, 4, 8192], P('blk', 'wide'), may hold values from -6 to 6
- lengths: int32 [8, 2304], P('blk', 'wide'), may hold values from 8192 to 32768
- owners: int32 [8, 2304], P('blk', 'wide'), may hold values from -1 to 767, as said below
- own_pick: int32 [8, 32, 8, 2, 4], P('blk', 'wide'), may hold values from 0 to 23
- visit_pick: int32 [8, 32, 8, 2, 4], P('blk', 'wide'), may hold values from 0 to 23
- pair_mask: int32 [8, 32, 8, 2, 4, 4], P('blk', 'wide'), may hold values 0 or 1
Outputs:
- correlations: float32 [8, 32, 8, 2, 4, 4, 1024], P('blk', 'wide')
Inputs may be any that keep to these rules, and one draw needn't show every extreme that they name: `owners`: in each group every station number 0 to 767 is named by exactly one slot. A device's valid slots come first and its other slots hold -1. The busiest device of each group fills all 72 slots and two devices hold none. At most 3 slots of one device name stations of one owner (stations w * 24 to w * 24 + 23 belong to owner w), and this most is reached in every group.
All inputs are finite; a program needn't handle non-finite values. No bound on the sum of `pair_mask` on one device may be relied on, other than what follows from the above.
Results may differ from a plain program's by a relative error of at most 0.0049.
Values may be sent and summed in bfloat16 or wider, within the bound.
No kernel may reach another device: no remote copies, remote signals or barrier semaphores. Data moves between devices by JAX's collectives and lax.ppermute only.
A program may use at most 192 MiB of HBM per device.

v0:
```python
import functools
import math

import jax
import jax.numpy as jnp
import numpy as np
from jax import lax
from jax.experimental import pallas as pl
from jax.experimental.pallas import tpu as pltpu
from jax.sharding import PartitionSpec as P

ST_DEV = 24
SEG = 4
NT = 8192
NF = 4096
LAGS = 1024
ROWS = 64
LANES = 128
BASE = 3
EXTRA = 3
SPILL = 12
LEN_BITS = 16
NOTES = 16
SMEM = pl.BlockSpec(memory_space=pltpu.SMEM)
VMEM = pl.BlockSpec(memory_space=pltpu.VMEM)
ANY = pl.BlockSpec(memory_space=pl.ANY)


def split_bf16(values):
    high = values.astype(jnp.bfloat16)
    low = (values - high.astype(np.float64)).astype(jnp.bfloat16)
    return high, low


def transform_tables():
    first = np.arange(ROWS)
    second = np.arange(LANES)
    half = np.arange(LANES // 2)
    angle = 2.0 * math.pi / ROWS * (first[:, None] * first[None, :] % ROWS)
    wave = np.concatenate([np.cos(angle), -np.sin(angle)], 0)
    wave = np.einsum("ab,kn->aknb", np.eye(2), wave).reshape(4 * ROWS, 2 * ROWS)
    first_table = np.concatenate(split_bf16(wave), 1)
    twist = 2.0 * math.pi / NT * (first[:, None] * second[None, :] % NT)
    twist_table = np.stack([np.cos(twist), np.sin(twist)]).astype(np.float32)
    angle = 2.0 * math.pi / LANES * (second[:, None] * half[None, :] % LANES)
    cos, sin = np.cos(angle), np.sin(angle)
    wave = np.concatenate([np.concatenate([cos, -sin], 1), np.concatenate([sin, cos], 1)], 0)
    second_table = np.concatenate(split_bf16(wave), 1)
    return first_table, twist_table, second_table


def lag_tables():
    row = np.arange(ROWS // 2, dtype=np.int64)
    lane = np.arange(LANES, dtype=np.int64)
    bins = (row[:, None] + ROWS // 2 * (lane // ROWS)) + ROWS * (lane % ROWS)
    bins = bins.reshape(-1)
    weight = np.where(bins == 0, 0.5, 1.0).astype(np.float32) / np.float32(math.sqrt(NF * SEG))

    def at(delay):
        phase = bins[:, None] * delay[None, :] % NT
        return phase.astype(np.float32) * np.float32(2.0 * math.pi / NT)

    ahead = at(np.arange(LAGS // 2, dtype=np.int64))
    edge = at(np.array([NT - LAGS // 2], dtype=np.int64))
    cos = weight[:, None] * np.cos(ahead)
    sin = -weight[:, None] * np.sin(ahead)
    sin[:, :1] = -weight[:, None] * np.sin(edge)
    last = (weight[:, None] * np.cos(edge)).reshape(ROWS // 2, 1, LANES)
    return (
        np.concatenate([cos, sin], 0).astype(jnp.bfloat16),
        last.astype(jnp.bfloat16).astype(np.float32),
    )


def owner_of(value):
    return ((value >> LEN_BITS) * 2731) >> 16


def unit(slot):
    return pl.ds(pl.multiple_of(slot * ROWS, ROWS), ROWS)


def spill_kernel(table, core_ref, own, same, other, plan, fill, notes, started, sem):
    core = core_ref[0]
    slots = table.shape[1]
    started[0] = 0

    @pl.loop(0, fill.shape[0])
    def _(dev):
        fill[dev] = 0
        for slot in range(BASE):
            notes[dev, slot] = -1

    for half in range(2):

        @pl.loop(0, slots)
        def _(at):
            value = table[half, at]
            plan[half, at] = -1

            @pl.when(value >= 0)
            def _():
                dev = owner_of(value)
                rank = fill[dev]
                fill[dev] = rank + 1

                @pl.when(rank < BASE)
                def _():
                    plan[half, at] = dev * 4 + rank
                    notes[dev, rank] = value - ((dev * ST_DEV) << LEN_BITS)

                @pl.when((rank >= BASE) & (core == half) & (started[0] < SPILL))
                def _():
                    index = started[0]
                    started[0] = index + 1
                    pltpu.make_async_copy(own.at[at, unit(core)], same.at[index], sem).start()
                    pltpu.make_async_copy(own.at[at, unit(1 - core)], other.at[index], sem).start()

    @pl.loop(0, 2 * started[0])
    def _(_):
        pltpu.make_async_copy(own.at[0, unit(0)], same.at[0], sem).wait()


def spill(wide_count, table, core, own):
    buffer = jax.ShapeDtypeStruct((SPILL, ROWS, LANES), jnp.bfloat16)
    return pl.pallas_call(
        spill_kernel,
        out_shape=(
            buffer,
            buffer,
            jax.ShapeDtypeStruct((2, table.shape[1]), jnp.int32),
            jax.ShapeDtypeStruct((wide_count,), jnp.int32),
            jax.ShapeDtypeStruct((wide_count, BASE), jnp.int32),
        ),
        in_specs=[SMEM, SMEM, ANY],
        out_specs=(VMEM, VMEM, SMEM, SMEM, SMEM),
        scratch_shapes=[pltpu.SMEM((1,), jnp.int32), pltpu.SemaphoreType.DMA],
        cost_estimate=pl.CostEstimate(flops=0, bytes_accessed=2**20, transcendentals=0),
        name="spill",
    )(table, core, own)


def route_kernel(table, plan, held, noted, guests, tiles, flag, fill, theirs, notes, taken):
    slots = plan.shape[1]
    devices = held.shape[0]
    flag[0] = 0

    @pl.loop(0, devices)
    def _(dev):
        fill[dev] = held[dev]
        theirs[dev] = 0
        for slot in range(BASE):
            notes[dev, slot] = noted[dev, slot]

    for half in range(2):
        for at in range(SPILL):
            guests[half, at] = -1

    for half in range(2):
        taken[0] = 0

        @pl.loop(0, slots)
        def _(at):
            value = table[2 + half, at]

            @pl.when(value >= 0)
            def _():
                dev = owner_of(value)
                rank = theirs[dev]
                theirs[dev] = rank + 1

                @pl.when(rank >= BASE)
                def _():
                    index = taken[0]
                    slot = fill[dev]
                    fits = (index < SPILL) & (slot < BASE)

                    @pl.when(fits)
                    def _():
                        fill[dev] = slot + 1
                        guests[half, index] = dev * 4 + slot
                        notes[dev, slot] = value - ((dev * ST_DEV) << LEN_BITS)

                    @pl.when(jnp.logical_not(fits))
                    def _():
                        flag[0] = 1

                    taken[0] = index + 1

    write_notes(tiles, 0, notes, flag[0])


def write_notes(out, begin, notes, flag):
    count = notes.shape[1]
    row = lax.broadcasted_iota(jnp.int32, (NOTES, LANES), 0)

    @pl.loop(0, notes.shape[0])
    def _(dev):
        tile = jnp.where(row == 4 * count, flag, 0)
        for slot in range(count):
            value = notes[dev, slot]
            tile = jnp.where(row == 4 * slot, (value >> LEN_BITS) + 1, tile)
            tile = jnp.where(row == 4 * slot + 1, (value & 0xFFFF) >> 8, tile)
            tile = jnp.where(row == 4 * slot + 2, value & 0xFF, tile)
        out[dev, begin : begin + NOTES, :] = tile.astype(jnp.float32).astype(jnp.bfloat16)


def route(table, plan, held, noted):
    devices = held.shape[0]
    return pl.pallas_call(
        route_kernel,
        out_shape=(
            jax.ShapeDtypeStruct((2, SPILL), jnp.int32),
            jax.ShapeDtypeStruct((devices, NOTES, LANES), jnp.bfloat16),
            jax.ShapeDtypeStruct((1,), jnp.int32),
        ),
        in_specs=[SMEM] * 4,
        out_specs=(SMEM, VMEM, SMEM),
        scratch_shapes=[
            pltpu.SMEM((devices,), jnp.int32),
            pltpu.SMEM((devices,), jnp.int32),
            pltpu.SMEM((devices, BASE), jnp.int32),
            pltpu.SMEM((1,), jnp.int32),
        ],
        cost_estimate=pl.CostEstimate(flops=0, bytes_accessed=2**18, transcendentals=0),
        name="route",
    )(table, plan, held, noted)


def pack_kernel(noted, plan, guests, core_ref, own, mate, same, other, *refs):
    tiles = refs[0] if noted else None
    out, flag, started, sem = refs[-4:]
    core = core_ref[0]
    started[0] = 0
    flag[0] = 0

    def place(codes, half, count, source, guest):
        @pl.loop(0, count)
        def _(at):
            code = codes[half, at]

            @pl.when(code >= 0)
            def _():
                started[0] += 1
                rows = source.at[at] if guest else source.at[at, unit(core)]
                pltpu.make_async_copy(rows, out.at[code >> 2, unit(code & 3)], sem).start()

    for half in range(2):

        @pl.when(core == half)
        def _():
            place(plan, half, plan.shape[1], own, False)
            place(guests, half, SPILL, same, True)

        @pl.when(core != half)
        def _():
            place(plan, half, plan.shape[1], mate, False)
            place(guests, half, SPILL, other, True)

    if noted:

        @pl.loop(0, out.shape[0])
        def _(dev):
            out[dev, BASE * ROWS :, :] = tiles[dev]

    @pl.loop(0, started[0])
    def _(_):
        pltpu.make_async_copy(own.at[0, unit(0)], out.at[0, unit(0)], sem).wait()


def pack(plan, guests, core, own, mate, same, other, tiles, after):
    wide_count = tiles.shape[0]
    noted = after is None
    last = tiles if noted else after
    return pl.pallas_call(
        functools.partial(pack_kernel, noted),
        out_shape=(
            jax.ShapeDtypeStruct((wide_count, BASE * ROWS + (NOTES if noted else 0), LANES), jnp.bfloat16),
            jax.ShapeDtypeStruct((1,), jnp.int32),
        ),
        in_specs=[SMEM, SMEM, SMEM, ANY, ANY, ANY, ANY, VMEM if noted else ANY],
        out_specs=(VMEM, SMEM),
        scratch_shapes=[pltpu.SMEM((1,), jnp.int32), pltpu.SemaphoreType.DMA],
        cost_estimate=pl.CostEstimate(flops=0, bytes_accessed=wide_count * BASE * NT * 4, transcendentals=0),
        name="pack",
    )(plan, guests, core, own, mate, same, other, last)


def late_kernel(table, core_ref, own, mate, out, fill, notes, started, sem):
    core = core_ref[0]
    started[0] = 0

    @pl.loop(0, out.shape[0])
    def _(dev):
        fill[dev] = 0
        for slot in range(EXTRA):
            notes[dev, slot] = -1

    def place(half, source):
        @pl.loop(0, table.shape[1])
        def _(at):
            value = table[half, at]

            @pl.when(value >= 0)
            def _():
                dev = owner_of(value)
                rank = fill[dev]
                fill[dev] = rank + 1

                @pl.when((rank >= BASE) & (rank < BASE + EXTRA))
                def _():
                    started[0] += 1
                    notes[dev, rank - BASE] = value - ((dev * ST_DEV) << LEN_BITS)
                    rows = source.at[at, unit(core)]
                    pltpu.make_async_copy(rows, out.at[dev, unit(rank - BASE)], sem).start()

    for half in range(2):

        @pl.when(core == half)
        def _():
            place(half, own)

        @pl.when(core != half)
        def _():
            place(half, mate)

    write_notes(out, EXTRA * ROWS, notes, 0)

    @pl.loop(0, started[0])
    def _(_):
        pltpu.make_async_copy(own.at[0, unit(0)], out.at[0, unit(0)], sem).wait()


def pack_late(wide_count, table, core, own, mate):
    return pl.pallas_call(
        late_kernel,
        out_shape=jax.ShapeDtypeStruct((wide_count, EXTRA * ROWS + NOTES, LANES), jnp.bfloat16),
        in_specs=[SMEM, SMEM, ANY, ANY],
        out_specs=VMEM,
        scratch_shapes=[
            pltpu.SMEM((wide_count,), jnp.int32),
            pltpu.SMEM((wide_count, EXTRA), jnp.int32),
            pltpu.SMEM((1,), jnp.int32),
            pltpu.SemaphoreType.DMA,
        ],
        cost_estimate=pl.CostEstimate(flops=0, bytes_accessed=wide_count * EXTRA * NT * 4, transcendentals=0),
        name="pack_late",
    )(table, core, own, mate)


def read_notes(rows, count):
    notes = rows[::2, count * ROWS :, 0].astype(jnp.float32).astype(jnp.int32)
    fields = notes[:, : 4 * count].reshape(-1, count, 4)
    station, length = fields[..., 0] - 1, fields[..., 1] * 256 + fields[..., 2]
    return station.reshape(-1), length.reshape(-1), notes[:, 4 * count]


def whiten_kernel(
    part, parts, source, length, picks, got, more, first, twist, second, *refs
):
    held, spectra, sem, sems = refs[-4:]
    stops, rows = picks.shape
    white = refs[-5 - parts]
    payload = refs[-4 - parts : -4]
    stations = held.shape[0]
    first_more = got.shape[0] // 2 * BASE
    batch = 8

    def fetch(rows, code, count, station):
        for seg in range(2):
            source_at = rows.at[2 * (code // count) + seg, unit(code % count)]
            pltpu.make_async_copy(source_at, held.at[station, unit(seg)], sems.at[station // batch]).start()

    @pl.loop(0, stations)
    def _(station):
        code = source[station]

        @pl.when(code < first_more)
        def _():
            fetch(got, code, BASE, station)

        @pl.when(code >= first_more)
        def _():
            fetch(more, code - first_more, EXTRA, station)

    row = lax.broadcasted_iota(jnp.int32, (2 * ROWS, LANES), 0)
    lane = lax.broadcasted_iota(jnp.int32, (2 * ROWS, LANES), 1)
    left = lax.broadcasted_iota(jnp.int32, (ROWS // 2, LANES), 1) < ROWS
    place = (2 * part + (row & 1)) * NT + (row >> 1) * LANES + lane

    def two_stations(station):
        sides = []
        for at in range(2):
            values = held[station + at].astype(jnp.float32)
            sides.append(jnp.where(place < length[station + at], values, 0.0).astype(jnp.bfloat16))
        values = jnp.concatenate(sides, 1)
        values = jnp.concatenate([values, values], 0)
        mixed = jnp.dot(first[...], values, preferred_element_type=jnp.float32)
        parts = []
        for at in range(2):
            for seg in range(2):
                real = mixed[2 * seg * ROWS : (2 * seg + 1) * ROWS, at * LANES : (at + 1) * LANES]
                imag = mixed[(2 * seg + 1) * ROWS : (2 * seg + 2) * ROWS, at * LANES : (at + 1) * LANES]
                turned_re = real * twist[0] + imag * twist[1]
                turned_im = imag * twist[0] - real * twist[1]
                parts.append(jnp.concatenate([turned_re, turned_im], 1))
        turned = jnp.concatenate(parts, 0)
        high = turned.astype(jnp.bfloat16)
        low = (turned - high.astype(jnp.float32)).astype(jnp.bfloat16)
        upper = jnp.dot(high, second[...], preferred_element_type=jnp.float32)
        lower = jnp.dot(low, second[:, :LANES], preferred_element_type=jnp.float32)
        spectrum = upper[:, :LANES] + (upper[:, LANES:] + lower)
        for at in range(2):
            for seg in range(2):
                begin = (2 * at + seg) * ROWS
                side = spectrum[begin : begin + ROWS]
                power = jnp.sum(side * side, axis=0, keepdims=True)
                power = (power + pltpu.roll(power, LANES // 2, 1)) * (1.0 / ROWS)
                scale = 1.0 / jnp.sqrt(power + 1e-06)
                side = side * scale
                upper, lower = side[: ROWS // 2], side[ROWS // 2 :]
                real = jnp.where(left, upper, pltpu.roll(lower, ROWS, 1))
                imag = jnp.where(left, pltpu.roll(upper, ROWS, 1), lower)
                spectra[station + at, seg, : ROWS // 2] = real.astype(jnp.bfloat16)
                spectra[station + at, seg, ROWS // 2 :] = imag.astype(jnp.bfloat16)

    @pl.loop(0, stations // batch)
    def _(at):
        these = held.at[pl.ds(at * batch, batch)]
        pltpu.make_async_copy(these, these, sems.at[at]).wait()
        for two in range(0, batch, 2):
            two_stations(batch * at + two)

    each = stops // parts
    for piece in range(parts):

        @pl.loop(0, each)
        def _(stop):
            for at in range(rows):
                row = spectra.at[picks[piece * each + stop, at]]
                pltpu.make_async_copy(row, payload[piece].at[stop, at], sem).start()

    whole = pltpu.make_async_copy(spectra, white, sems.at[0])
    whole.start()
    for piece in range(parts):
        pltpu.make_async_copy(payload[piece], payload[piece], sem).wait()
    whole.wait()


def whiten(part, parts, source, length, picks, got, more, tables, after):
    stops, rows = picks.shape
    piece = jax.ShapeDtypeStruct((stops // parts, rows, 2, ROWS, LANES), jnp.bfloat16)
    return pl.pallas_call(
        functools.partial(whiten_kernel, part, parts),
        out_shape=(jax.ShapeDtypeStruct((ST_DEV, 2, ROWS, LANES), jnp.bfloat16),) + (piece,) * parts,
        in_specs=[SMEM, SMEM, SMEM, ANY, ANY, VMEM, VMEM, VMEM] + [ANY] * len(after),
        out_specs=(ANY,) * (1 + parts),
        scratch_shapes=[
            pltpu.VMEM((ST_DEV, 2 * ROWS, LANES), jnp.bfloat16),
            pltpu.VMEM((ST_DEV, 2, ROWS, LANES), jnp.bfloat16),
            pltpu.SemaphoreType.DMA,
            pltpu.SemaphoreType.DMA((ST_DEV // 8,)),
        ],
        cost_estimate=pl.CostEstimate(
            flops=2 * ST_DEV * 2 * ROWS * 256 * 400, bytes_accessed=4 * 1024 * 1024, transcendentals=0
        ),
        name="whiten",
    )(source, length, picks, got, more, *tables, *after)


def cross_rows(near_pick, near, far, cross, fresh, ready):
    stops, rows = near_pick.shape
    side = rows // 2
    step = 16
    half = ROWS // 2

    @pl.loop(0, stops)
    def _(stop):
        ready(stop)
        for two in range(2):
            first = two * side
            own = [near_pick[stop, first + i] for i in range(side)]

            @pl.loop(0, half // step)
            def _(chunk):
                real = pl.ds(pl.multiple_of(chunk * step, step), step)
                imag = pl.ds(pl.multiple_of(half + chunk * step, step), step)

                def both(ref, row):
                    return [
                        (ref[row, s, real, :].astype(jnp.float32), ref[row, s, imag, :].astype(jnp.float32))
                        for s in range(2)
                    ]

                here = [both(near, own[i]) for i in range(side)]
                for j in range(side):
                    there = both(far.at[stop], first + j)
                    for i in range(side):
                        pair = ((stop * 2 + two) * side + i) * side + j
                        total_re = sum(n[0] * f[0] + n[1] * f[1] for n, f in zip(here[i], there))
                        total_im = sum(n[1] * f[0] - n[0] * f[1] for n, f in zip(here[i], there))
                        for total, add in ((total_re, 0), (total_im, half)):
                            at = pl.ds(pl.multiple_of(pair * ROWS + add + chunk * step, step), step)
                            if fresh:
                                cross[at, :] = total
                            else:
                                cross[at, :] += total


def lag_kernel(stops, near_pick, far_at, white_a, home, *refs):
    far_a = refs[: stops - 1]
    white_b, far_b, table, last, mask, result, near, far, cross, out, tables, sem, sems, table_sem = refs[stops - 1 :]
    pairs = out.shape[0]
    copies = [pltpu.make_async_copy(white, near.at[part], sem.at[part]) for part, white in enumerate((white_a, white_b))]
    copies[0].start()
    pltpu.make_async_copy(home, far.at[0, 0], sems.at[0, 0]).start()
    for stop in range(1, stops):
        pltpu.make_async_copy(far_a[stop - 1], far.at[0, stop], sems.at[0, stop]).start()
    copies[1].start()
    for stop in range(stops):
        pltpu.make_async_copy(far_b.at[far_at[stop]], far.at[1, stop], sems.at[1, stop]).start()
    load_table = pltpu.make_async_copy(table, tables, table_sem)
    load_table.start()
    for part in range(2):

        def ready(stop):
            pltpu.make_async_copy(far.at[part, stop], far.at[part, stop], sems.at[part, stop]).wait()

        copies[part].wait()
        cross_rows(near_pick, near.at[part], far.at[part], cross, part == 0, ready)
    load_table.wait()
    group = 8
    depth = group * LANES
    half = LAGS // 2
    turns = ROWS // 2 // group

    def product(turn, edge):
        base = turn * group
        slabs = [
            cross[pl.ds(base + k, pairs, stride=ROWS), :].astype(jnp.bfloat16) for k in range(group)
        ]
        if edge is not None:
            for k in range(group):
                edge += slabs[k].astype(jnp.float32) * last[base + k]
        part = jnp.dot(
            jnp.concatenate(slabs, 1),
            tables[pl.ds(pl.multiple_of(base * LANES, depth), depth), :],
            preferred_element_type=jnp.float32,
        )
        return part, edge

    out[:, :half] = jnp.zeros((pairs, half), jnp.float32)
    out[:, half:] = jnp.zeros((pairs, half), jnp.float32)

    def even_step(turn, edge):
        part, edge = product(turn, edge)
        out[:, :half] += part
        return edge

    edge = lax.fori_loop(0, turns, even_step, jnp.zeros((pairs, LANES), jnp.float32))

    @pl.loop(turns, 2 * turns)
    def _(turn):
        out[:, half:] += product(turn, None)[0]

    edge = jnp.sum(edge, axis=1, keepdims=True)
    lane = lax.broadcasted_iota(jnp.int32, (pairs, LANES), 1)
    mirror = (LANES - lane) % LANES
    first = lane == 0
    listed = mask[...]
    count = half // LANES
    before, after = [], []
    for block in range(count):
        even = out[:, block * LANES : (block + 1) * LANES]
        odd = out[:, half + block * LANES : half + (block + 1) * LANES]
        if block == 0:
            edge = edge + odd
            odd = jnp.where(first, 0.0, odd)
        before.append(even - odd)
        after.append(even + odd)
    for block in range(count):
        turned = jnp.take_along_axis(before[count - 1 - block], mirror, axis=1)
        start = edge if block == 0 else before[count - block]
        lags = pl.ds(block * LANES, LANES)
        result[:, :, lags] = (jnp.where(first, start, turned) * listed).reshape(result.shape[:2] + (LANES,))
        lags = pl.ds(half + block * LANES, LANES)
        result[:, :, lags] = (after[block] * listed).reshape(result.shape[:2] + (LANES,))


def lagged(near_pick, far_at, white_a, home, far_a, white_b, far_b, table, last, mask):
    pairs = mask.shape[0]
    stops, rows = near_pick.shape
    side = rows // 2
    return pl.pallas_call(
        functools.partial(lag_kernel, stops),
        out_shape=jax.ShapeDtypeStruct((pairs // side, side, LAGS), jnp.float32),
        in_specs=[SMEM, SMEM] + [ANY] * (stops + 4) + [VMEM, VMEM],
        out_specs=VMEM,
        scratch_shapes=[
            pltpu.VMEM((2,) + white_a.shape, jnp.bfloat16),
            pltpu.VMEM((2,) + far_b.shape, jnp.bfloat16),
            pltpu.VMEM((pairs * ROWS, LANES), jnp.float32),
            pltpu.VMEM((pairs, LAGS), jnp.float32),
            pltpu.VMEM(table.shape, jnp.bfloat16),
            pltpu.SemaphoreType.DMA((2,)),
            pltpu.SemaphoreType.DMA((2, stops)),
            pltpu.SemaphoreType.DMA,
        ],
        compiler_params=pltpu.CompilerParams(vmem_limit_bytes=60 * 1024 * 1024),
        cost_estimate=pl.CostEstimate(
            flops=2 * pairs * NF * LAGS, bytes_accessed=16 * 1024 * 1024, transcendentals=0
        ),
        name="lagged",
    )(near_pick, far_at, white_a, home, *far_a, white_b, far_b, table, last, mask)


def empty(shape):
    return pl.pallas_call(
        lambda out: None,
        out_shape=jax.ShapeDtypeStruct(shape, jnp.bfloat16),
        out_specs=ANY,
        name="empty",
    )()


def on_device(records, lengths, owners, own_pick, visit_pick, pair_mask):
    wide_count = lax.axis_size("wide")
    stops = lax.axis_size("blk")
    column = lax.axis_index("wide")
    group = lax.axis_index("blk")
    core = column % 2
    slots = records.shape[1]
    steps = jnp.arange(stops, dtype=jnp.int32)
    core_at = core.reshape(1)

    def across(shard, bits):
        return lax.ppermute(shard, "wide", [(i, i ^ bits) for i in range(wide_count)])

    over = wide_count // 2
    packed = jnp.where(owners[0] >= 0, (owners[0] << LEN_BITS) + lengths[0], -1)
    others = [across(packed, bits) for bits in (1, over, over + 1)]
    table = jnp.where(
        core == 0,
        jnp.stack([packed, others[0], others[1], others[2]]),
        jnp.stack([others[0], packed, others[2], others[1]]),
    )

    blocks = records[0].reshape(slots, SEG, ROWS, LANES)

    def halves(part):
        return blocks[:, 2 * part : 2 * part + 2].transpose(0, 2, 1, 3).reshape(slots, 2 * ROWS, LANES)

    def send(payload):
        return lax.all_to_all(payload, "wide", split_axis=0, concat_axis=0, tiled=True)

    own_a = halves(0)
    mate_a = across(own_a, 1)
    same_a, other_a, plan, held, noted = spill(wide_count, table, core_at, own_a)
    same_a, other_a = across(same_a, over), across(other_a, over + 1)
    guests, tiles, _ = route(table, plan, held, noted)
    load_a, flag_a = pack(plan, guests, core_at, own_a, mate_a, same_a, other_a, tiles, None)
    got_a = send(load_a)
    own_b = jnp.where(flag_a[0] >= 0, halves(1), 0.0)
    mate_b = across(own_b, 1)
    same_b, other_b, *_ = spill(wide_count, table, core_at, own_b)
    same_b, other_b = across(same_b, over), across(other_b, over + 1)
    visits = jnp.where(flag_a[0] >= 0, visit_pick[0, 0].reshape(stops, -1), 0)
    by_stop = jnp.stack(
        [visits[0]]
        + [
            lax.ppermute(visits[stop], "blk", [(i, (i - stop) % stops) for i in range(stops)])
            for stop in range(1, stops)
        ]
    )
    load_b, _ = pack(plan, guests, core_at, own_b, mate_b, same_b, other_b, tiles, by_stop)
    got_b = send(load_b)
    by_dest = by_stop[(steps - group) % stops]

    station, length, spilled = read_notes(got_a, BASE)
    spilled = jnp.max(spilled) > 0

    def late():
        rows = [
            send(pack_late(wide_count, table, core_at, own, mate))
            for own, mate in ((own_a, mate_a), (own_b, mate_b))
        ]
        return (rows[0], rows[1]) + read_notes(rows[0], EXTRA)[:2]

    def never():
        rows = [empty((wide_count, EXTRA * ROWS + NOTES, LANES)) for _ in range(2)]
        count = wide_count // 2 * EXTRA
        return rows[0], rows[1], jnp.full((count,), -1, jnp.int32), jnp.zeros((count,), jnp.int32)

    more_a, more_b, more_station, more_length = lax.cond(spilled, late, never)
    station = jnp.concatenate([station, more_station])
    length = jnp.concatenate([length, more_length])
    chosen = station[None, :] == jnp.arange(ST_DEV, dtype=jnp.int32)[:, None]
    codes = jnp.arange(station.shape[0], dtype=jnp.int32)
    source = jnp.max(jnp.where(chosen, codes[None], 0), axis=1)
    length = jnp.max(jnp.where(chosen, length[None], 0), axis=1)

    tables = [jnp.asarray(table) for table in transform_tables()]
    near_pick = own_pick[0, 0].reshape(stops, -1)
    white_a, home, *payload_a = whiten(0, stops, source, length, by_stop, got_a, more_a, tables, [])
    far_a = [
        lax.ppermute(payload_a[stop - 1][0], "blk", [(i, (i + stop) % stops) for i in range(stops)])
        for stop in range(1, stops)
    ]
    white_b, payload_b = whiten(1, 1, source, length, by_dest, got_b, more_b, tables, far_a)
    far_b = lax.all_to_all(payload_b, "blk", split_axis=0, concat_axis=0, tiled=True)

    far_at = (group - steps) % stops
    mask = pair_mask[0, 0].astype(jnp.float32).reshape(-1, 1)
    lags, last = lag_tables()
    result = lagged(near_pick, far_at, white_a, home[0], far_a, white_b, far_b, jnp.asarray(lags), jnp.asarray(last), mask)
    return result.reshape((1, 1) + pair_mask.shape[2:] + (LAGS,))


def solution(mesh):
    return jax.shard_map(
        on_device,
        mesh=mesh,
        in_specs=(
            P("blk", "wide", None, None),
            P("blk", "wide"),
            P("blk", "wide"),
            P("blk", "wide", None, None, None),
            P("blk", "wide", None, None, None),
            P("blk", "wide", None, None, None, None),
        ),
        out_specs=P("blk", "wide", None, None, None, None, None),
        check_vma=False,
    )
```

profile of v0, /device:TPU:1, one launch (start us, length us, event | category | flops | bytes accessed | tf_op | source)
XLA Modules:
  0.0 213.3 jit_solution(1001682216873880271)
XLA Ops:
  0.0 4.5 %slice.96 = bf16[72,2,64,128]{3,1,2,0:T(2,128)(2,1)S(1)} slice(bf16[72,4,64,128]{3,1,2,0:T(4,128)(2,1)} %bitcast.50), slice={[0:72], [0:2], [0:64], [0:128]} | slice | bytes 4718592 | tf_op jit(solution)/shard_map/slice | solution.py:651
  4.5 3.3 %collective-permute-start.3 = (bf16[72,128,128]{2,1,0:T(8,128)(2,1)S(1)}, bf16[72,128,128]{2,1,0:T(8,128)(2,1)}, u32[]{:S(2)}, u32[]{:S(2)}) collective-permute-start(bf16[72,128,128]{2,1,0:T(8,128)(2,1)S(1)} %bitcast.46), channel_id=1, source_target_pairs={{0,8},{8,0},{16,24},{24,16},{32,40},{40,32},{48,56},{56,48},{64,72... | collective-permute-start | bytes 7077896 | tf_op jit(solution)/shard_map/ppermute | solution.py:637
  7.9 1.4 collective-permute-start.1
  12.0 4.6 %spill.2 = (bf16[12,64,128]{2,1,0:T(8,128)(2,1)}, bf16[12,64,128]{2,1,0:T(8,128)(2,1)}, s32[2,72]{1,0:T(2,128)}, s32[32]{0:T(128)}, s32[32,3]{1,0:T(8,128)}) custom-call(s32[4,72]{1,0:T(4,128)S(1)} %add_select_fusion.table, s32[1]{0:T(128)} %bitcast.5.core_ref, bf16[72,128,128]{2,1,0:T(8,128)(2,1)S(1)} %bitcast.47), custom_call_target="tpu_custom_call" | custom-call | bytes 1048576 | tf_op jit(solution)/shard_map/spill/pallas_call | solution.py:126
  16.7 2.0 collective-permute-start.5
  18.6 6.1 %route.1 = (s32[2,12]{1,0:T(2,128)}, bf16[32,16,128]{2,1,0:T(8,128)(2,1)}, s32[1]{0:T(128)}) custom-call(s32[4,72]{1,0:T(4,128)S(1)} %add_select_fusion.table, s32[2,72]{1,0:T(2,128)} %get-tuple-element.50.plan, s32[32]{0:T(128)} %get-tuple-element.51.held, s32[32,3]{1,0:T(8,128)} %get-tuple-element.52.noted), custom_call_target="tpu_custom_call" | custom-call | bytes 262144 | tf_op jit(solution)/shard_map/route/pallas_call | solution.py:210
  24.8 2.9 %collective-permute-done.5.other = bf16[12,64,128]{2,1,0:T(8,128)(2,1)S(1)} collective-permute-done((bf16[12,64,128]{2,1,0:T(8,128)(2,1)}, bf16[12,64,128]{2,1,0:T(8,128)(2,1)S(1)}, u32[]{:S(2)}, u32[]{:S(2)}) %collective-permute-start.5) | collective-permute-done | bytes 196640 | tf_op jit(solution)/shard_map/ppermute | solution.py:637
  28.4 5.5 %pack.2 = (bf16[32,208,128]{2,1,0:T(8,128)(2,1)}, s32[1]{0:T(128)}) custom-call(s32[2,72]{1,0:T(2,128)} %get-tuple-element.50.plan, s32[2,12]{1,0:T(2,128)} %get-tuple-element.53.guests, s32[1]{0:T(128)} %bitcast.5.core_ref, bf16[72,128,128]{2,1,0:T(8,128)(2,1)S(1)} %bitcast.48, bf16[72,128,128]{2,1,0:T(8,128)(2,1)} %collective-permute-done.3.mate, ...), custom_call_target="tpu_custom_call" | custom-call | bytes 3145728 | tf_op jit(solution)/shard_map/pack/pallas_call | solution.py:275
  33.9 8.7 %all-to-all-start.2 = ((bf16[32,208,128]{2,1,0:T(8,128)(2,1)}), bf16[32,208,128]{2,1,0:T(8,128)(2,1)}, u32[]{:S(2)}, u32[]{:S(2)}) async-start(bf16[32,208,128]{2,1,0:T(8,128)(2,1)} %get-tuple-element.57), calls=%async_computation.2 | async-start | bytes 3407872 | tf_op jit(solution)/shard_map/all_to_all | solution.py:654
  43.3 7.4 %broadcast_select_fusion = bf16[72,2,64,128]{3,1,2,0:T(2,128)(2,1)} fusion(pred[]{:T(512)} %bitcast.10, bf16[72,4,64,128]{3,1,2,0:T(4,128)(2,1)} %bitcast.51), kind=kLoop, calls=%fused_computation.5 | loop fusion | flops 1179648 | bytes 4718593 | tf_op jit(solution)/shard_map/jit(_where)/select_n | solution.py:663
  51.0 4.8 %spill.3 = (bf16[12,64,128]{2,1,0:T(8,128)(2,1)}, bf16[12,64,128]{2,1,0:T(8,128)(2,1)}, s32[2,72]{1,0:T(2,128)}, s32[32]{0:T(128)}, s32[32,3]{1,0:T(8,128)}) custom-call(s32[4,72]{1,0:T(4,128)S(1)} %add_select_fusion.table, s32[1]{0:T(128)} %bitcast.5.core_ref, bf16[72,128,128]{2,1,0:T(8,128)(2,1)} %bitcast.12.own), custom_call_target="tpu_custom_call" | custom-call | bytes 1048576 | tf_op jit(solution)/shard_map/spill/pallas_call | solution.py:126
  55.8 1.5 collective-permute-start.21
  58.3 5.0 %collective-permute-start.7 = (s32[8]{0:T(128)S(1)}, s32[8]{0:T(128)S(1)}, u32[]{:S(2)}, u32[]{:S(2)}) collective-permute-start(s32[8]{0:T(128)S(1)} %squeeze.60), channel_id=1, source_target_pairs={{0,7},{1,0},{2,1},{3,2},{4,3},{5,4},{6,5},{7,6},{8,15},{9,8},{10,9... | collective-permute-start | bytes 104 | tf_op jit(solution)/shard_map/ppermute | solution.py:671
  64.5 3.3 %collective-permute-done.8 = s32[8]{0:T(128)S(1)} collective-permute-done((s32[8]{0:T(128)S(1)}, s32[8]{0:T(128)S(1)}, u32[]{:S(2)}, u32[]{:S(2)}) %collective-permute-start.8) | collective-permute-done | bytes 64 | tf_op jit(solution)/shard_map/ppermute | solution.py:671
  68.1 3.0 %collective-permute-start.11 = (s32[8]{0:T(128)S(1)}, s32[8]{0:T(128)S(1)}, u32[]{:S(2)}, u32[]{:S(2)}) collective-permute-start(s32[8]{0:T(128)S(1)} %squeeze.64), channel_id=1, source_target_pairs={{0,3},{1,4},{2,5},{3,6},{4,7},{5,0},{6,1},{7,2},{8,11},{9,12},{10,... | collective-permute-start | bytes 104 | tf_op jit(solution)/shard_map/ppermute | solution.py:671
  71.1 4.2 %collective-permute-done.10 = s32[8]{0:T(128)S(1)} collective-permute-done((s32[8]{0:T(128)S(1)}, s32[8]{0:T(128)S(1)}, u32[]{:S(2)}, u32[]{:S(2)}) %collective-permute-start.10) | collective-permute-done | bytes 64 | tf_op jit(solution)/shard_map/ppermute | solution.py:671
  75.3 2.4 %collective-permute-start.12 = (s32[8]{0:T(128)S(1)}, s32[8]{0:T(128)S(1)}, u32[]{:S(2)}, u32[]{:S(2)}) collective-permute-start(s32[8]{0:T(128)S(1)} %squeeze.65), channel_id=1, source_target_pairs={{0,2},{1,3},{2,4},{3,5},{4,6},{5,7},{6,0},{7,1},{8,10},{9,11},{10,... | collective-permute-start | bytes 104 | tf_op jit(solution)/shard_map/ppermute | solution.py:671
  77.8 1.5 collective-permute-start.13
  79.3 2.6 %collective-permute-done.12 = s32[8]{0:T(128)S(1)} collective-permute-done((s32[8]{0:T(128)S(1)}, s32[8]{0:T(128)S(1)}, u32[]{:S(2)}, u32[]{:S(2)}) %collective-permute-start.12) | collective-permute-done | bytes 64 | tf_op jit(solution)/shard_map/ppermute | solution.py:671
  81.9 1.9 collective-permute-done.13
  85.8 3.9 %pack.3 = (bf16[32,192,128]{2,1,0:T(8,128)(2,1)}, s32[1]{0:T(128)}) custom-call(s32[2,72]{1,0:T(2,128)} %get-tuple-element.50.plan, s32[2,12]{1,0:T(2,128)} %get-tuple-element.53.guests, s32[1]{0:T(128)} %bitcast.5.core_ref, bf16[72,128,128]{2,1,0:T(8,128)(2,1)} %bitcast.12.own, bf16[72,128,128]{2,1,0:T(8,128)(2,1)} %collective-permute-done.6.mate, ...), custom_call_target="tpu_custom_call" | custom-call | bytes 3145728 | tf_op jit(solution)/shard_map/pack/pallas_call | solution.py:275
  92.3 10.2 %all-to-all-start.3 = ((bf16[32,192,128]{2,1,0:T(8,128)(2,1)}), bf16[32,192,128]{2,1,0:T(8,128)(2,1)S(1)}, u32[]{:S(2)}, u32[]{:S(2)}) async-start(bf16[32,192,128]{2,1,0:T(8,128)(2,1)} %get-tuple-element.73), calls=%async_computation.3 | async-start | bytes 3145728 | tf_op jit(solution)/shard_map/all_to_all | solution.py:654
  103.8 7.6 %whiten.2 = (bf16[24,2,64,128]{3,2,1,0:T(8,128)(2,1)}, bf16[1,8,2,64,128]{4,3,2,1,0:T(8,128)(2,1)}, bf16[1,8,2,64,128]{4,3,2,1,0:T(8,128)(2,1)}, bf16[1,8,2,64,1...) custom-call(s32[24]{0:T(128)} %get-tuple-element.86.source, ...), custom_call_target="tpu_custom_call" | custom-call | flops 629145600 | bytes 4194304 | tf_op jit(solution)/shard_map/whiten/pallas_call | solution.py:453
  111.6 3.1 %collective-permute-start.16 = (bf16[8,2,64,128]{3,2,1,0:T(8,128)(2,1)}, bf16[8,2,64,128]{3,2,1,0:T(8,128)(2,1)S(1)}, u32[]{:S(2)}, u32[]{:S(2)}) collective-permute-start(bf16[8,2,64,128]{3,2,1,0:T(8,128)(2,1)} %bitcast.73), channel_id=1, source_target_pairs={{0,3},{1,4},{2,5},{3,6},{4,7},{5,0},{6,1},{7,2},{8,11},{9,12},{10,... | collective-permute-start | bytes 786440 | tf_op jit(solution)/shard_map/ppermute | solution.py:706
  114.7 2.2 %collective-permute-start.17 = (bf16[8,2,64,128]{3,2,1,0:T(8,128)(2,1)}, bf16[8,2,64,128]{3,2,1,0:T(8,128)(2,1)S(1)}, u32[]{:S(2)}, u32[]{:S(2)}) collective-permute-start(bf16[8,2,64,128]{3,2,1,0:T(8,128)(2,1)} %bitcast.72), channel_id=1, source_target_pairs={{0,4},{1,5},{2,6},{3,7},{4,0},{5,1},{6,2},{7,3},{8,12},{9,13},{10,... | collective-permute-start | bytes 786440 | tf_op jit(solution)/shard_map/ppermute | solution.py:706
  118.0 22.4 %collective-permute-done.14.refs_0_ = bf16[8,2,64,128]{3,2,1,0:T(8,128)(2,1)S(1)} collective-permute-done((bf16[8,2,64,128]{3,2,1,0:T(8,128)(2,1)}, bf16[8,2,64,128]{3,2,1,0:T(8,128)(2,1)S(1)}, u32[]{:S(2)}, u32[]{:S(2)}) %collective-permute-start.14) | collective-permute-done | bytes 262176 | tf_op jit(solution)/shard_map/ppermute | solution.py:706
  143.1 7.4 %collective-permute-done.17.refs_3_ = bf16[8,2,64,128]{3,2,1,0:T(8,128)(2,1)S(1)} collective-permute-done((bf16[8,2,64,128]{3,2,1,0:T(8,128)(2,1)}, bf16[8,2,64,128]{3,2,1,0:T(8,128)(2,1)S(1)}, u32[]{:S(2)}, u32[]{:S(2)}) %collective-permute-start.17) | collective-permute-done | bytes 262176 | tf_op jit(solution)/shard_map/ppermute | solution.py:706
  150.5 1.6 collective-permute-done.20.refs_6_
  153.3 7.6 %whiten.3 = (bf16[24,2,64,128]{3,2,1,0:T(8,128)(2,1)}, bf16[8,8,2,64,128]{4,3,2,1,0:T(8,128)(2,1)}) custom-call(s32[24]{0:T(128)} %get-tuple-element.86.source, s32[24]{0:T(128)} %get-tuple-element.85.length, s32[8,8]{1,0:T(8,128)} %gather_fusion, bf16[32,192,128]{2,1,0:T(8,128)(2,1)} %copy-done.1, bf16[32,208,128]{2,1,0:T(8,128)(2,1)} %get-tuple-element.74.more, ...), custom_call_target="tpu_custom_call" | custom-call | flops 629145600 | bytes 4194304 | tf_op jit(solution)/shard_map/whiten/pallas_call | solution.py:453
  161.0 6.3 %all-to-all-start.4 = ((bf16[8,8,2,64,128]{4,3,2,1,0:T(8,128)(2,1)}), bf16[8,8,2,64,128]{4,3,2,1,0:T(8,128)(2,1)S(1)}, u32[]{:S(2)}, u32[]{:S(2)}) async-start(bf16[8,8,2,64,128]{4,3,2,1,0:T(8,128)(2,1)} %get-tuple-element.76), calls=%async_computation.4 | async-start | bytes 4194304 | tf_op jit(solution)/shard_map/all_to_all | solution.py:710
  169.4 26.4 %all-to-all-done.4.refs_8_ = bf16[8,8,2,64,128]{4,3,2,1,0:T(8,128)(2,1)S(1)} async-done(((bf16[8,8,2,64,128]{4,3,2,1,0:T(8,128)(2,1)}), bf16[8,8,2,64,128]{4,3,2,1,0:T(8,128)(2,1)S(1)}, u32[]{:S(2)}, u32[]{:S(2)}) %all-to-all-start.4) | async-done | bytes 2097184 | tf_op jit(solution)/shard_map/all_to_all | solution.py:710
  197.1 16.0 %lagged.1 = f32[64,4,1024]{2,1,0:T(4,128)} custom-call(s32[8,8]{1,0:T(8,128)} %copy.42.near_pick, s32[8]{0:T(128)} %and_select_fusion.1.far_at, bf16[24,2,64,128]{3,2,1,0:T(8,128)(2,1)} %get-tuple-element.62.white_a, bf16[8,2,64,128]{3,2,1,0:T(8,128)(2,1)} %bitcast.52, bf16[8,2,64,128]{3,2,1,0:T(8,128)(2,1)} %copy-done.2, bf16[8,2,64,128]{3,2,1,0:T(8,128)(2,1)} %copy-done.3, ...), custom_call_target="tpu_custom_call" | custom-call | flops 2147483648 | bytes 16777216 | tf_op jit(solution)/shard_map/lagged/pallas_call | solution.py:594
  (105 shorter events, 20.0 us)
Async XLA Ops:
  0.0 7.8 %copy-start.17 = (s32[1,72]{1,0:T(1,128)S(1)}, s32[1,72]{1,0:T(1,128)}, u32[]{:S(2)}) copy-start(s32[1,72]{1,0:T(1,128)} %param.15) | copy-start | bytes 868
  0.0 7.8 %copy-start.18 = (s32[1,72]{1,0:T(1,128)S(1)}, s32[1,72]{1,0:T(1,128)}, u32[]{:S(2)}) copy-start(s32[1,72]{1,0:T(1,128)} %param.14) | copy-start | bytes 868
  4.5 23.2 %collective-permute-start.3 = (bf16[72,128,128]{2,1,0:T(8,128)(2,1)S(1)}, bf16[72,128,128]{2,1,0:T(8,128)(2,1)}, u32[]{:S(2)}, u32[]{:S(2)}) collective-permute-start(bf16[72,128,128]{2,1,0:T(8,128)(2,1)S(1)} %bitcast.46), channel_id=1, source_target_pairs={{0,8},{8,0},{16,24},{24,16},{32,40},{40,32},{48,56},{56,48},{64,72... | collective-permute-start | bytes 7077896 | tf_op jit(solution)/shard_map/ppermute | solution.py:637
  7.8 3.1 %collective-permute-start.2 = (s32[72]{0:T(128)S(1)}, s32[72]{0:T(128)S(1)}, u32[]{:S(2)}, u32[]{:S(2)}) collective-permute-start(s32[72]{0:T(128)S(1)} %bitcast.58), channel_id=1, source_target_pairs={{0,136},{8,128},{16,152},{24,144},{32,168},{40,160},{48,184},{56,1... | collective-permute-start | bytes 872 | tf_op jit(solution)/shard_map/ppermute | solution.py:637
  7.9 3.0 %collective-permute-start.1 = (s32[72]{0:T(128)S(1)}, s32[72]{0:T(128)S(1)}, u32[]{:S(2)}, u32[]{:S(2)}) collective-permute-start(s32[72]{0:T(128)S(1)} %bitcast.59), channel_id=1, source_target_pairs={{0,128},{8,136},{16,144},{24,152},{32,160},{40,168},{48,176},{56,1... | collective-permute-start | bytes 872 | tf_op jit(solution)/shard_map/ppermute | solution.py:637
  9.3 2.7 %collective-permute-start = (s32[72]{0:T(128)S(1)}, s32[72]{0:T(128)S(1)}, u32[]{:S(2)}, u32[]{:S(2)}) collective-permute-start(s32[72]{0:T(128)S(1)} %bitcast.60), channel_id=1, source_target_pairs={{0,8},{8,0},{16,24},{24,16},{32,40},{40,32},{48,56},{56,48},{64,72... | collective-permute-start | bytes 872 | tf_op jit(solution)/shard_map/ppermute | solution.py:637
  16.6 8.2 %collective-permute-start.4 = (bf16[12,64,128]{2,1,0:T(8,128)(2,1)}, bf16[12,64,128]{2,1,0:T(8,128)(2,1)S(1)}, u32[]{:S(2)}, u32[]{:S(2)}) collective-permute-start(bf16[12,64,128]{2,1,0:T(8,128)(2,1)} %get-tuple-element.54), channel_id=1, source_target_pairs={{0,128},{8,136},{16,144},{24,152},{32,160},{40,168},{48,176},{56,1... | collective-permute-start | bytes 589832 | tf_op jit(solution)/shard_map/ppermute | solution.py:637
  16.7 11.0 %collective-permute-start.5 = (bf16[12,64,128]{2,1,0:T(8,128)(2,1)}, bf16[12,64,128]{2,1,0:T(8,128)(2,1)S(1)}, u32[]{:S(2)}, u32[]{:S(2)}) collective-permute-start(bf16[12,64,128]{2,1,0:T(8,128)(2,1)} %get-tuple-element.55), channel_id=1, source_target_pairs={{0,136},{8,128},{16,152},{24,144},{32,168},{40,160},{48,184},{56,1... | collective-permute-start | bytes 589832 | tf_op jit(solution)/shard_map/ppermute | solution.py:637
  33.9 55.8 %all-to-all-start.2 = ((bf16[32,208,128]{2,1,0:T(8,128)(2,1)}), bf16[32,208,128]{2,1,0:T(8,128)(2,1)}, u32[]{:S(2)}, u32[]{:S(2)}) async-start(bf16[32,208,128]{2,1,0:T(8,128)(2,1)} %get-tuple-element.57), calls=%async_computation.2 | async-start | bytes 3407872 | tf_op jit(solution)/shard_map/all_to_all | solution.py:654
  50.7 33.7 %collective-permute-start.6 = (bf16[72,128,128]{2,1,0:T(8,128)(2,1)}, bf16[72,128,128]{2,1,0:T(8,128)(2,1)}, u32[]{:S(2)}, u32[]{:S(2)}) collective-permute-start(bf16[72,128,128]{2,1,0:T(8,128)(2,1)} %bitcast.12.own), channel_id=1, source_target_pairs={{0,8},{8,0},{16,24},{24,16},{32,40},{40,32},{48,56},{56,48},{64,72... | collective-permute-start | bytes 7077896 | tf_op jit(solution)/shard_map/ppermute | solution.py:637
  55.8 28.6 %collective-permute-start.21 = (bf16[12,64,128]{2,1,0:T(8,128)(2,1)}, bf16[12,64,128]{2,1,0:T(8,128)(2,1)S(1)}, u32[]{:S(2)}, u32[]{:S(2)}) collective-permute-start(bf16[12,64,128]{2,1,0:T(8,128)(2,1)} %get-tuple-element.71), channel_id=1, source_target_pairs={{0,128},{8,136},{16,144},{24,152},{32,160},{40,168},{48,176},{56,1... | collective-permute-start | bytes 589832 | tf_op jit(solution)/shard_map/ppermute | solution.py:637
  57.3 27.1 %collective-permute-start.22 = (bf16[12,64,128]{2,1,0:T(8,128)(2,1)}, bf16[12,64,128]{2,1,0:T(8,128)(2,1)S(1)}, u32[]{:S(2)}, u32[]{:S(2)}) collective-permute-start(bf16[12,64,128]{2,1,0:T(8,128)(2,1)} %get-tuple-element.72), channel_id=1, source_target_pairs={{0,136},{8,128},{16,152},{24,144},{32,168},{40,160},{48,184},{56,1... | collective-permute-start | bytes 589832 | tf_op jit(solution)/shard_map/ppermute | solution.py:637
  58.3 5.7 %collective-permute-start.7 = (s32[8]{0:T(128)S(1)}, s32[8]{0:T(128)S(1)}, u32[]{:S(2)}, u32[]{:S(2)}) collective-permute-start(s32[8]{0:T(128)S(1)} %squeeze.60), channel_id=1, source_target_pairs={{0,7},{1,0},{2,1},{3,2},{4,3},{5,4},{6,5},{7,6},{8,15},{9,8},{10,9... | collective-permute-start | bytes 104 | tf_op jit(solution)/shard_map/ppermute | solution.py:671
  63.4 4.3 %collective-permute-start.8 = (s32[8]{0:T(128)S(1)}, s32[8]{0:T(128)S(1)}, u32[]{:S(2)}, u32[]{:S(2)}) collective-permute-start(s32[8]{0:T(128)S(1)} %squeeze.61), channel_id=1, source_target_pairs={{0,6},{1,7},{2,0},{3,1},{4,2},{5,3},{6,4},{7,5},{8,14},{9,15},{10,... | collective-permute-start | bytes 104 | tf_op jit(solution)/shard_map/ppermute | solution.py:671
  64.1 4.0 %collective-permute-start.9 = (s32[8]{0:T(128)S(1)}, s32[8]{0:T(128)S(1)}, u32[]{:S(2)}, u32[]{:S(2)}) collective-permute-start(s32[8]{0:T(128)S(1)} %squeeze.62), channel_id=1, source_target_pairs={{0,5},{1,6},{2,7},{3,0},{4,1},{5,2},{6,3},{7,4},{8,13},{9,14},{10,... | collective-permute-start | bytes 104 | tf_op jit(solution)/shard_map/ppermute | solution.py:671
  67.7 7.6 %collective-permute-start.10 = (s32[8]{0:T(128)S(1)}, s32[8]{0:T(128)S(1)}, u32[]{:S(2)}, u32[]{:S(2)}) collective-permute-start(s32[8]{0:T(128)S(1)} %squeeze.63), channel_id=1, source_target_pairs={{0,4},{1,5},{2,6},{3,7},{4,0},{5,1},{6,2},{7,3},{8,12},{9,13},{10,... | collective-permute-start | bytes 104 | tf_op jit(solution)/shard_map/ppermute | solution.py:671
  68.1 9.7 %collective-permute-start.11 = (s32[8]{0:T(128)S(1)}, s32[8]{0:T(128)S(1)}, u32[]{:S(2)}, u32[]{:S(2)}) collective-permute-start(s32[8]{0:T(128)S(1)} %squeeze.64), channel_id=1, source_target_pairs={{0,3},{1,4},{2,5},{3,6},{4,7},{5,0},{6,1},{7,2},{8,11},{9,12},{10,... | collective-permute-start | bytes 104 | tf_op jit(solution)/shard_map/ppermute | solution.py:671
  75.3 6.6 %collective-permute-start.12 = (s32[8]{0:T(128)S(1)}, s32[8]{0:T(128)S(1)}, u32[]{:S(2)}, u32[]{:S(2)}) collective-permute-start(s32[8]{0:T(128)S(1)} %squeeze.65), channel_id=1, source_target_pairs={{0,2},{1,3},{2,4},{3,5},{4,6},{5,7},{6,0},{7,1},{8,10},{9,11},{10,... | collective-permute-start | bytes 104 | tf_op jit(solution)/shard_map/ppermute | solution.py:671
  77.8 6.0 %collective-permute-start.13 = (s32[8]{0:T(128)S(1)}, s32[8]{0:T(128)S(1)}, u32[]{:S(2)}, u32[]{:S(2)}) collective-permute-start(s32[8]{0:T(128)S(1)} %squeeze.66), channel_id=1, source_target_pairs={{0,1},{1,2},{2,3},{3,4},{4,5},{5,6},{6,7},{7,0},{8,9},{9,10},{10,1... | collective-permute-start | bytes 104 | tf_op jit(solution)/shard_map/ppermute | solution.py:671
  92.3 59.8 %all-to-all-start.3 = ((bf16[32,192,128]{2,1,0:T(8,128)(2,1)}), bf16[32,192,128]{2,1,0:T(8,128)(2,1)S(1)}, u32[]{:S(2)}, u32[]{:S(2)}) async-start(bf16[32,192,128]{2,1,0:T(8,128)(2,1)} %get-tuple-element.73), calls=%async_computation.3 | async-start | bytes 3145728 | tf_op jit(solution)/shard_map/all_to_all | solution.py:654
  103.8 36.7 %copy-start.9 = (s32[8,8]{1,0:T(8,128)S(1)}, s32[8,8]{1,0:T(8,128)}, u32[]{:S(2)}) copy-start(s32[8,8]{1,0:T(8,128)} %stack.56.picks.refs_0_) | copy-start | bytes 772
  111.4 29.0 %collective-permute-start.14 = (bf16[8,2,64,128]{3,2,1,0:T(8,128)(2,1)}, bf16[8,2,64,128]{3,2,1,0:T(8,128)(2,1)S(1)}, u32[]{:S(2)}, u32[]{:S(2)}) collective-permute-start(bf16[8,2,64,128]{3,2,1,0:T(8,128)(2,1)} %bitcast.75), channel_id=1, source_target_pairs={{0,1},{1,2},{2,3},{3,4},{4,5},{5,6},{6,7},{7,0},{8,9},{9,10},{10,1... | collective-permute-start | bytes 786440 | tf_op jit(solution)/shard_map/ppermute | solution.py:706
  111.5 28.9 %collective-permute-start.15 = (bf16[8,2,64,128]{3,2,1,0:T(8,128)(2,1)}, bf16[8,2,64,128]{3,2,1,0:T(8,128)(2,1)S(1)}, u32[]{:S(2)}, u32[]{:S(2)}) collective-permute-start(bf16[8,2,64,128]{3,2,1,0:T(8,128)(2,1)} %bitcast.74), channel_id=1, source_target_pairs={{0,2},{1,3},{2,4},{3,5},{4,6},{5,7},{6,0},{7,1},{8,10},{9,11},{10,... | collective-permute-start | bytes 786440 | tf_op jit(solution)/shard_map/ppermute | solution.py:706
  111.6 31.5 %collective-permute-start.16 = (bf16[8,2,64,128]{3,2,1,0:T(8,128)(2,1)}, bf16[8,2,64,128]{3,2,1,0:T(8,128)(2,1)S(1)}, u32[]{:S(2)}, u32[]{:S(2)}) collective-permute-start(bf16[8,2,64,128]{3,2,1,0:T(8,128)(2,1)} %bitcast.73), channel_id=1, source_target_pairs={{0,3},{1,4},{2,5},{3,6},{4,7},{5,0},{6,1},{7,2},{8,11},{9,12},{10,... | collective-permute-start | bytes 786440 | tf_op jit(solution)/shard_map/ppermute | solution.py:706
  114.7 35.8 %collective-permute-start.17 = (bf16[8,2,64,128]{3,2,1,0:T(8,128)(2,1)}, bf16[8,2,64,128]{3,2,1,0:T(8,128)(2,1)S(1)}, u32[]{:S(2)}, u32[]{:S(2)}) collective-permute-start(bf16[8,2,64,128]{3,2,1,0:T(8,128)(2,1)} %bitcast.72), channel_id=1, source_target_pairs={{0,4},{1,5},{2,6},{3,7},{4,0},{5,1},{6,2},{7,3},{8,12},{9,13},{10,... | collective-permute-start | bytes 786440 | tf_op jit(solution)/shard_map/ppermute | solution.py:706
  116.9 33.6 %collective-permute-start.18 = (bf16[8,2,64,128]{3,2,1,0:T(8,128)(2,1)}, bf16[8,2,64,128]{3,2,1,0:T(8,128)(2,1)S(1)}, u32[]{:S(2)}, u32[]{:S(2)}) collective-permute-start(bf16[8,2,64,128]{3,2,1,0:T(8,128)(2,1)} %bitcast.71), channel_id=1, source_target_pairs={{0,5},{1,6},{2,7},{3,0},{4,1},{5,2},{6,3},{7,4},{8,13},{9,14},{10,... | collective-permute-start | bytes 786440 | tf_op jit(solution)/shard_map/ppermute | solution.py:706
  140.4 11.7 %copy-start.2 = (bf16[8,2,64,128]{3,2,1,0:T(8,128)(2,1)}, bf16[8,2,64,128]{3,2,1,0:T(8,128)(2,1)S(1)}, u32[]{:S(2)}) copy-start(bf16[8,2,64,128]{3,2,1,0:T(8,128)(2,1)S(1)} %collective-permute-done.14.refs_0_) | copy-start | bytes 786436
  140.4 10.1 %collective-permute-start.19 = (bf16[8,2,64,128]{3,2,1,0:T(8,128)(2,1)}, bf16[8,2,64,128]{3,2,1,0:T(8,128)(2,1)S(1)}, u32[]{:S(2)}, u32[]{:S(2)}) collective-permute-start(bf16[8,2,64,128]{3,2,1,0:T(8,128)(2,1)} %bitcast.70), channel_id=1, source_target_pairs={{0,6},{1,7},{2,0},{3,1},{4,2},{5,3},{6,4},{7,5},{8,14},{9,15},{10,... | collective-permute-start | bytes 786440 | tf_op jit(solution)/shard_map/ppermute | solution.py:706
  140.4 11.7 %copy-start.3 = (bf16[8,2,64,128]{3,2,1,0:T(8,128)(2,1)}, bf16[8,2,64,128]{3,2,1,0:T(8,128)(2,1)S(1)}, u32[]{:S(2)}) copy-start(bf16[8,2,64,128]{3,2,1,0:T(8,128)(2,1)S(1)} %collective-permute-done.15.refs_1_) | copy-start | bytes 786436
  140.4 11.7 %collective-permute-start.20 = (bf16[8,2,64,128]{3,2,1,0:T(8,128)(2,1)}, bf16[8,2,64,128]{3,2,1,0:T(8,128)(2,1)S(1)}, u32[]{:S(2)}, u32[]{:S(2)}) collective-permute-start(bf16[8,2,64,128]{3,2,1,0:T(8,128)(2,1)} %bitcast.69), channel_id=1, source_target_pairs={{0,7},{1,0},{2,1},{3,2},{4,3},{5,4},{6,5},{7,6},{8,15},{9,8},{10,9... | collective-permute-start | bytes 786440 | tf_op jit(solution)/shard_map/ppermute | solution.py:706
  143.1 9.1 %copy-start.4 = (bf16[8,2,64,128]{3,2,1,0:T(8,128)(2,1)}, bf16[8,2,64,128]{3,2,1,0:T(8,128)(2,1)S(1)}, u32[]{:S(2)}) copy-start(bf16[8,2,64,128]{3,2,1,0:T(8,128)(2,1)S(1)} %collective-permute-done.16.refs_2_) | copy-start | bytes 786436
  161.0 34.8 %all-to-all-start.4 = ((bf16[8,8,2,64,128]{4,3,2,1,0:T(8,128)(2,1)}), bf16[8,8,2,64,128]{4,3,2,1,0:T(8,128)(2,1)S(1)}, u32[]{:S(2)}, u32[]{:S(2)}) async-start(bf16[8,8,2,64,128]{4,3,2,1,0:T(8,128)(2,1)} %get-tuple-element.76), calls=%async_computation.4 | async-start | bytes 4194304 | tf_op jit(solution)/shard_map/all_to_all | solution.py:710
  (13 other events, 33.5 us)
where the time goes:
time: 216 us; the launch traced here: 213 us
  waiting for transfers between devices  76.7 us (36%)
  Pallas kernels  56.1 us (26%)
  starting transfers between devices  54 us (25%)
  local copies, waits for them, and re-layouts  13.9 us (6%)
  other arithmetic  10.8 us (5%)
    ppermute x7, waiting for transfers between devices, on_device(): lax.ppermute(payload_a[stop - 1][0], 'blk', [(i, (i + stop) % stops) for...  32.8 us
    all_to_all x1, waiting for transfers between devices, on_device(): lax.all_to_all(payload_b, 'blk', split_axis=0, concat_axis=0, tiled=True)  26.4 us
    all_to_all x2, starting transfers between devices, send(): lax.all_to_all(payload, 'wide', split_axis=0, concat_axis=0, tiled=True)  19 us
    pallas_call x1, Pallas kernels, lagged(): pl.pallas_call(functools.partial(lag_kernel, stops), out_shape=jax.ShapeD...  16 us
    pallas_call x2, Pallas kernels, whiten(): pl.pallas_call(functools.partial(whiten_kernel, part, parts), out_shape=(...  15.2 us
    ppermute x7, waiting for transfers between devices, on_device(): lax.ppermute(visits[stop], 'blk', [(i, (i - stop) % stops) for i in range...  12.6 us
    ppermute x7, starting transfers between devices, on_device(): lax.ppermute(visits[stop], 'blk', [(i, (i - stop) % stops) for i in range...  12.4 us
    ppermute x9, starting transfers between devices, across(): lax.ppermute(shard, 'wide', [(i, i ^ bits) for i in range(wide_count)])  9.82 us
  transfers between devices with their start and end apart: 26, of which 14 were waited for; matrix products, arithmetic and copies ran while one was open for 6% of the time, Pallas kernels for 13%

commit v1 on v0

--- a/solution.py
+++ b/solution.py
@@ -16,8 +16,8 @@
 LAGS = 1024
 ROWS = 64
 LANES = 128
-BASE = 3
-EXTRA = 3
+MOST = 6
+SLOTS = (4, 3)
 SPILL = 12
 LEN_BITS = 16
 NOTES = 16
@@ -80,23 +80,23 @@
     return pl.ds(pl.multiple_of(slot * ROWS, ROWS), ROWS)
 
 
-def spill_kernel(table, core_ref, own, same, other, plan, fill, notes, started, sem):
+def rows_kernel(low, count, noted, table, core_ref, own, mate, *refs):
+    base = refs[0] if noted else None
+    out, flag, fill, notes, started, sem = refs[-6:]
     core = core_ref[0]
-    slots = table.shape[1]
     started[0] = 0
-
-    @pl.loop(0, fill.shape[0])
+    flag[0] = 0
+
+    @pl.loop(0, out.shape[0])
     def _(dev):
         fill[dev] = 0
-        for slot in range(BASE):
+        for slot in range(count):
             notes[dev, slot] = -1
 
-    for half in range(2):
-
-        @pl.loop(0, slots)
+    def place(half, source):
+        @pl.loop(0, table.shape[1])
         def _(at):
             value = table[half, at]
-            plan[half, at] = -1
 
             @pl.when(value >= 0)
             def _():
@@ -104,12 +104,94 @@
                 rank = fill[dev]
                 fill[dev] = rank + 1
 
-                @pl.when(rank < BASE)
+                @pl.when((rank >= low) & (rank < low + count))
+                def _():
+                    started[0] += 1
+                    notes[dev, rank - low] = value - ((dev * ST_DEV) << LEN_BITS)
+                    rows = source.at[at, unit(core)]
+                    pltpu.make_async_copy(rows, out.at[dev, unit(rank - low)], sem).start()
+
+                @pl.when(rank >= low + count)
+                def _():
+                    flag[0] = 1
+
+    for half in range(2):
+
+        @pl.when(core == half)
+        def _():
+            place(half, own)
+
+        @pl.when(core != half)
+        def _():
+            place(half, mate)
+
+    if noted:
+        row = lax.broadcasted_iota(jnp.int32, (NOTES, LANES), 0)
+        table_rows = base[...]
+
+        @pl.loop(0, out.shape[0])
+        def _(dev):
+            tile = jnp.where(row == 3 * count, flag[0], table_rows)
+            for slot in range(count):
+                value = notes[dev, slot]
+                tile = jnp.where(row == 3 * slot, (value >> LEN_BITS) + 1, tile)
+                tile = jnp.where(row == 3 * slot + 1, (value & 0xFFFF) >> 8, tile)
+                tile = jnp.where(row == 3 * slot + 2, value & 0xFF, tile)
+            out[dev, count * ROWS :, :] = tile.astype(jnp.float32).astype(jnp.bfloat16)
+
+    @pl.loop(0, started[0])
+    def _(_):
+        pltpu.make_async_copy(own.at[0, unit(0)], out.at[0, unit(0)], sem).wait()
+
+
+def pack_rows(low, count, wide_count, table, core, own, mate, base):
+    noted = base is not None
+    return pl.pallas_call(
+        functools.partial(rows_kernel, low, count, noted),
+        out_shape=(
+            jax.ShapeDtypeStruct((wide_count, count * ROWS + (NOTES if noted else 0), LANES), jnp.bfloat16),
+            jax.ShapeDtypeStruct((1,), jnp.int32),
+        ),
+        in_specs=[SMEM, SMEM, ANY, ANY] + [VMEM] * noted,
+        out_specs=(VMEM, SMEM),
+        scratch_shapes=[
+            pltpu.SMEM((wide_count,), jnp.int32),
+            pltpu.SMEM((wide_count, count), jnp.int32),
+            pltpu.SMEM((1,), jnp.int32),
+            pltpu.SemaphoreType.DMA,
+        ],
+        cost_estimate=pl.CostEstimate(flops=0, bytes_accessed=wide_count * count * NT * 4, transcendentals=0),
+        name="pack_rows",
+    )(table, core, own, mate, *([base] * noted))
+
+
+def spill_kernel(base, table, core_ref, own, same, other, plan, fill, started, sem):
+    core = core_ref[0]
+    slots = table.shape[1]
+    started[0] = 0
+
+    @pl.loop(0, fill.shape[0])
+    def _(dev):
+        fill[dev] = 0
+
+    for half in range(2):
+
+        @pl.loop(0, slots)
+        def _(at):
+            value = table[half, at]
+            plan[half, at] = -1
+
+            @pl.when(value >= 0)
+            def _():
+                dev = owner_of(value)
+                rank = fill[dev]
+                fill[dev] = rank + 1
+
+                @pl.when(rank < base)
                 def _():
                     plan[half, at] = dev * 4 + rank
-                    notes[dev, rank] = value - ((dev * ST_DEV) << LEN_BITS)
-
-                @pl.when((rank >= BASE) & (core == half) & (started[0] < SPILL))
+
+                @pl.when((rank >= base) & (core == half) & (started[0] < SPILL))
                 def _():
                     index = started[0]
                     started[0] = index + 1
@@ -121,45 +203,47 @@
         pltpu.make_async_copy(own.at[0, unit(0)], same.at[0], sem).wait()
 
 
-def spill(wide_count, table, core, own):
+def spill(base, wide_count, table, core, own):
     buffer = jax.ShapeDtypeStruct((SPILL, ROWS, LANES), jnp.bfloat16)
     return pl.pallas_call(
-        spill_kernel,
+        functools.partial(spill_kernel, base),
         out_shape=(
             buffer,
             buffer,
             jax.ShapeDtypeStruct((2, table.shape[1]), jnp.int32),
             jax.ShapeDtypeStruct((wide_count,), jnp.int32),
-            jax.ShapeDtypeStruct((wide_count, BASE), jnp.int32),
         ),
         in_specs=[SMEM, SMEM, ANY],
-        out_specs=(VMEM, VMEM, SMEM, SMEM, SMEM),
+        out_specs=(VMEM, VMEM, SMEM, SMEM),
         scratch_shapes=[pltpu.SMEM((1,), jnp.int32), pltpu.SemaphoreType.DMA],
         cost_estimate=pl.CostEstimate(flops=0, bytes_accessed=2**20, transcendentals=0),
         name="spill",
     )(table, core, own)
 
 
-def route_kernel(table, plan, held, noted, guests, tiles, flag, fill, theirs, notes, taken):
-    slots = plan.shape[1]
-    devices = held.shape[0]
-    flag[0] = 0
-
-    @pl.loop(0, devices)
+def pack_kernel(base, table, plan, held, core_ref, own, mate, same, other, after, out, fill, theirs, started, taken, sem):
+    core = core_ref[0]
+    started[0] = 0
+
+    @pl.loop(0, out.shape[0])
     def _(dev):
         fill[dev] = held[dev]
         theirs[dev] = 0
-        for slot in range(BASE):
-            notes[dev, slot] = noted[dev, slot]
-
-    for half in range(2):
-        for at in range(SPILL):
-            guests[half, at] = -1
-
-    for half in range(2):
+
+    def place(half, source, guests):
+        @pl.loop(0, plan.shape[1])
+        def _(at):
+            code = plan[half, at]
+
+            @pl.when(code >= 0)
+            def _():
+                started[0] += 1
+                rows = source.at[at, unit(core)]
+                pltpu.make_async_copy(rows, out.at[code >> 2, unit(code & 3)], sem).start()
+
         taken[0] = 0
 
-        @pl.loop(0, slots)
+        @pl.loop(0, plan.shape[1])
         def _(at):
             value = table[2 + half, at]
 
@@ -169,190 +253,100 @@
                 rank = theirs[dev]
                 theirs[dev] = rank + 1
 
-                @pl.when(rank >= BASE)
+                @pl.when(rank >= base)
                 def _():
                     index = taken[0]
                     slot = fill[dev]
-                    fits = (index < SPILL) & (slot < BASE)
-
-                    @pl.when(fits)
+                    taken[0] = index + 1
+
+                    @pl.when((index < SPILL) & (slot < base))
                     def _():
                         fill[dev] = slot + 1
-                        guests[half, index] = dev * 4 + slot
-                        notes[dev, slot] = value - ((dev * ST_DEV) << LEN_BITS)
-
-                    @pl.when(jnp.logical_not(fits))
-                    def _():
-                        flag[0] = 1
-
-                    taken[0] = index + 1
-
-    write_notes(tiles, 0, notes, flag[0])
-
-
-def write_notes(out, begin, notes, flag):
-    count = notes.shape[1]
-    row = lax.broadcasted_iota(jnp.int32, (NOTES, LANES), 0)
-
-    @pl.loop(0, notes.shape[0])
-    def _(dev):
-        tile = jnp.where(row == 4 * count, flag, 0)
-        for slot in range(count):
-            value = notes[dev, slot]
-            tile = jnp.where(row == 4 * slot, (value >> LEN_BITS) + 1, tile)
-            tile = jnp.where(row == 4 * slot + 1, (value & 0xFFFF) >> 8, tile)
-            tile = jnp.where(row == 4 * slot + 2, value & 0xFF, tile)
-        out[dev, begin : begin + NOTES, :] = tile.astype(jnp.float32).astype(jnp.bfloat16)
-
-
-def route(table, plan, held, noted):
-    devices = held.shape[0]
-    return pl.pallas_call(
-        route_kernel,
-        out_shape=(
-            jax.ShapeDtypeStruct((2, SPILL), jnp.int32),
-            jax.ShapeDtypeStruct((devices, NOTES, LANES), jnp.bfloat16),
-            jax.ShapeDtypeStruct((1,), jnp.int32),
-        ),
-        in_specs=[SMEM] * 4,
-        out_specs=(SMEM, VMEM, SMEM),
-        scratch_shapes=[
-            pltpu.SMEM((devices,), jnp.int32),
-            pltpu.SMEM((devices,), jnp.int32),
-            pltpu.SMEM((devices, BASE), jnp.int32),
-            pltpu.SMEM((1,), jnp.int32),
-        ],
-        cost_estimate=pl.CostEstimate(flops=0, bytes_accessed=2**18, transcendentals=0),
-        name="route",
-    )(table, plan, held, noted)
-
-
-def pack_kernel(noted, plan, guests, core_ref, own, mate, same, other, *refs):
-    tiles = refs[0] if noted else None
-    out, flag, started, sem = refs[-4:]
-    core = core_ref[0]
-    started[0] = 0
-    flag[0] = 0
-
-    def place(codes, half, count, source, guest):
-        @pl.loop(0, count)
-        def _(at):
-            code = codes[half, at]
-
-            @pl.when(code >= 0)
-            def _():
-                started[0] += 1
-                rows = source.at[at] if guest else source.at[at, unit(core)]
-                pltpu.make_async_copy(rows, out.at[code >> 2, unit(code & 3)], sem).start()
+                        started[0] += 1
+                        pltpu.make_async_copy(guests.at[index], out.at[dev, unit(slot)], sem).start()
 
     for half in range(2):
 
         @pl.when(core == half)
         def _():
-            place(plan, half, plan.shape[1], own, False)
-            place(guests, half, SPILL, same, True)
+            place(half, own, same)
 
         @pl.when(core != half)
         def _():
-            place(plan, half, plan.shape[1], mate, False)
-            place(guests, half, SPILL, other, True)
-
-    if noted:
-
-        @pl.loop(0, out.shape[0])
-        def _(dev):
-            out[dev, BASE * ROWS :, :] = tiles[dev]
+            place(half, mate, other)
 
     @pl.loop(0, started[0])
     def _(_):
         pltpu.make_async_copy(own.at[0, unit(0)], out.at[0, unit(0)], sem).wait()
 
 
-def pack(plan, guests, core, own, mate, same, other, tiles, after):
-    wide_count = tiles.shape[0]
-    noted = after is None
-    last = tiles if noted else after
+def pack_planned(base, table, plan, held, core, own, mate, same, other, after):
+    wide_count = held.shape[0]
     return pl.pallas_call(
-        functools.partial(pack_kernel, noted),
-        out_shape=(
-            jax.ShapeDtypeStruct((wide_count, BASE * ROWS + (NOTES if noted else 0), LANES), jnp.bfloat16),
-            jax.ShapeDtypeStruct((1,), jnp.int32),
-        ),
-        in_specs=[SMEM, SMEM, SMEM, ANY, ANY, ANY, ANY, VMEM if noted else ANY],
-        out_specs=(VMEM, SMEM),
-        scratch_shapes=[pltpu.SMEM((1,), jnp.int32), pltpu.SemaphoreType.DMA],
-        cost_estimate=pl.CostEstimate(flops=0, bytes_accessed=wide_count * BASE * NT * 4, transcendentals=0),
-        name="pack",
-    )(plan, guests, core, own, mate, same, other, last)
-
-
-def late_kernel(table, core_ref, own, mate, out, fill, notes, started, sem):
-    core = core_ref[0]
-    started[0] = 0
-
-    @pl.loop(0, out.shape[0])
-    def _(dev):
-        fill[dev] = 0
-        for slot in range(EXTRA):
-            notes[dev, slot] = -1
-
-    def place(half, source):
-        @pl.loop(0, table.shape[1])
-        def _(at):
-            value = table[half, at]
-
-            @pl.when(value >= 0)
-            def _():
-                dev = owner_of(value)
-                rank = fill[dev]
-                fill[dev] = rank + 1
-
-                @pl.when((rank >= BASE) & (rank < BASE + EXTRA))
-                def _():
-                    started[0] += 1
-                    notes[dev, rank - BASE] = value - ((dev * ST_DEV) << LEN_BITS)
-                    rows = source.at[at, unit(core)]
-                    pltpu.make_async_copy(rows, out.at[dev, unit(rank - BASE)], sem).start()
-
-    for half in range(2):
-
-        @pl.when(core == half)
-        def _():
-            place(half, own)
-
-        @pl.when(core != half)
-        def _():
-            place(half, mate)
-
-    write_notes(out, EXTRA * ROWS, notes, 0)
-
-    @pl.loop(0, started[0])
-    def _(_):
-        pltpu.make_async_copy(own.at[0, unit(0)], out.at[0, unit(0)], sem).wait()
-
-
-def pack_late(wide_count, table, core, own, mate):
-    return pl.pallas_call(
-        late_kernel,
-        out_shape=jax.ShapeDtypeStruct((wide_count, EXTRA * ROWS + NOTES, LANES), jnp.bfloat16),
-        in_specs=[SMEM, SMEM, ANY, ANY],
+        functools.partial(pack_kernel, base),
+        out_shape=jax.ShapeDtypeStruct((wide_count, base * ROWS, LANES), jnp.bfloat16),
+        in_specs=[SMEM] * 4 + [ANY] * 5,
         out_specs=VMEM,
         scratch_shapes=[
             pltpu.SMEM((wide_count,), jnp.int32),
-            pltpu.SMEM((wide_count, EXTRA), jnp.int32),
+            pltpu.SMEM((wide_count,), jnp.int32),
+            pltpu.SMEM((1,), jnp.int32),
             pltpu.SMEM((1,), jnp.int32),
             pltpu.SemaphoreType.DMA,
         ],
-        cost_estimate=pl.CostEstimate(flops=0, bytes_accessed=wide_count * EXTRA * NT * 4, transcendentals=0),
-        name="pack_late",
-    )(table, core, own, mate)
-
-
-def read_notes(rows, count):
-    notes = rows[::2, count * ROWS :, 0].astype(jnp.float32).astype(jnp.int32)
-    fields = notes[:, : 4 * count].reshape(-1, count, 4)
+        cost_estimate=pl.CostEstimate(flops=0, bytes_accessed=wide_count * base * NT * 4, transcendentals=0),
+        name="pack_planned",
+    )(table, plan, held, core, own, mate, same, other, after)
+
+
+def table_notes(packed):
+    owner = (packed >> LEN_BITS) + 1
+    length = jnp.where(packed >= 0, packed & 0xFFFF, 0)
+    parts = jnp.concatenate([owner >> 8, owner & 0xFF, length >> 8, length & 0xFF])
+    rows = 3 * LANES - parts.shape[0]
+    parts = jnp.pad(parts, (0, rows)).reshape(3, LANES)
+    return jnp.pad(parts, ((NOTES - 3, 0), (0, 0)))
+
+
+def read_slots(rows, count):
+    notes = rows[::2, count * ROWS : count * ROWS + 3 * count + 1, 0].astype(jnp.float32).astype(jnp.int32)
+    fields = notes[:, : 3 * count].reshape(-1, count, 3)
     station, length = fields[..., 0] - 1, fields[..., 1] * 256 + fields[..., 2]
-    return station.reshape(-1), length.reshape(-1), notes[:, 4 * count]
+    return station.reshape(-1), length.reshape(-1), notes[:, 3 * count]
+
+
+def read_table(rows, slots, chips):
+    parts = rows[:, -3:, :].astype(jnp.float32).astype(jnp.int32)
+    parts = parts.reshape(rows.shape[0], -1)[:, : 4 * slots].reshape(chips, 2, 4, slots)
+    return (parts[:, :, 0] * 256 + parts[:, :, 1] - 1).reshape(chips, 2 * slots)
+
+
+def second_places(owner, column, base):
+    chips, entries = owner.shape
+    extra = MOST - base
+    slots = entries // 2
+    listed = owner >= 0
+    dev = jnp.where(listed, owner // ST_DEV, -1)
+    order = jnp.arange(entries, dtype=jnp.int32)
+    earlier = order[None, :] < order[:, None]
+    alike = (dev[:, :, None] == dev[:, None, :]) & earlier
+    rank = jnp.sum(alike.astype(jnp.int32), axis=2)
+    over = listed & (rank >= base)
+    near = earlier & (order[None, :] // slots == order[:, None] // slots)
+    index = jnp.sum((over[:, None, :] & near).astype(jnp.int32), axis=2)
+    sent = over & (index < SPILL)
+    guest = jnp.sum((alike & sent[:, None, :]).astype(jnp.int32), axis=2)
+    host_dev = jnp.concatenate([dev[chips // 2 :], dev[: chips // 2]])
+    host_held = jnp.sum((dev[:, :, None] == host_dev[:, None, :]).astype(jnp.int32), axis=2)
+    slot = host_held + guest
+    fits = sent & (slot < base)
+    chip = jnp.arange(chips, dtype=jnp.int32)[:, None]
+    host = (chip + chips // 2) % chips
+    code = jnp.where(rank < base, chip * base + rank, chips * base + chip * extra + rank - base)
+    code = jnp.where(fits, host * base + slot, code)
+    local = column * ST_DEV + jnp.arange(ST_DEV, dtype=jnp.int32)
+    chosen = owner[None] == local[:, None, None]
+    return jnp.sum(jnp.where(chosen, code[None], 0), axis=(1, 2)), jnp.any(over & jnp.logical_not(fits))
 
 
 def whiten_kernel(
@@ -363,7 +357,8 @@
     white = refs[-5 - parts]
     payload = refs[-4 - parts : -4]
     stations = held.shape[0]
-    first_more = got.shape[0] // 2 * BASE
+    base = SLOTS[part]
+    first_more = got.shape[0] // 2 * base
     batch = 8
 
     def fetch(rows, code, count, station):
@@ -377,11 +372,11 @@
 
         @pl.when(code < first_more)
         def _():
-            fetch(got, code, BASE, station)
+            fetch(got, code, base, station)
 
         @pl.when(code >= first_more)
         def _():
-            fetch(more, code - first_more, EXTRA, station)
+            fetch(more, code - first_more, MOST - base, station)
 
     row = lax.broadcasted_iota(jnp.int32, (2 * ROWS, LANES), 0)
     lane = lax.broadcasted_iota(jnp.int32, (2 * ROWS, LANES), 1)
@@ -655,58 +650,62 @@
 
     own_a = halves(0)
     mate_a = across(own_a, 1)
-    same_a, other_a, plan, held, noted = spill(wide_count, table, core_at, own_a)
-    same_a, other_a = across(same_a, over), across(other_a, over + 1)
-    guests, tiles, _ = route(table, plan, held, noted)
-    load_a, flag_a = pack(plan, guests, core_at, own_a, mate_a, same_a, other_a, tiles, None)
+    base_a, base_b = SLOTS
+    load_a, flag_a = pack_rows(0, base_a, wide_count, table, core_at, own_a, mate_a, table_notes(packed))
     got_a = send(load_a)
     own_b = jnp.where(flag_a[0] >= 0, halves(1), 0.0)
     mate_b = across(own_b, 1)
-    same_b, other_b, *_ = spill(wide_count, table, core_at, own_b)
+    same_b, other_b, plan, held = spill(base_b, wide_count, table, core_at, own_b)
     same_b, other_b = across(same_b, over), across(other_b, over + 1)
-    visits = jnp.where(flag_a[0] >= 0, visit_pick[0, 0].reshape(stops, -1), 0)
-    by_stop = jnp.stack(
-        [visits[0]]
-        + [
-            lax.ppermute(visits[stop], "blk", [(i, (i - stop) % stops) for i in range(stops)])
-            for stop in range(1, stops)
-        ]
-    )
-    load_b, _ = pack(plan, guests, core_at, own_b, mate_b, same_b, other_b, tiles, by_stop)
+    visits = jnp.where(flag_a[0] >= 0, visit_pick[0, 0].reshape(1, stops, -1), 0)
+    bit = 1
+    while bit < stops:
+        theirs = lax.ppermute(visits, "blk", [(i, i ^ bit) for i in range(stops)])
+        upper = (group // bit) % 2 == 1
+        visits = jnp.concatenate([jnp.where(upper, theirs, visits), jnp.where(upper, visits, theirs)])
+        bit *= 2
+    by_dest = visits[steps, (steps - group) % stops]
+    by_stop = by_dest[(steps + group) % stops]
+    load_b = pack_planned(base_b, table, plan, held, core_at, own_b, mate_b, same_b, other_b, by_stop)
     got_b = send(load_b)
-    by_dest = by_stop[(steps - group) % stops]
-
-    station, length, spilled = read_notes(got_a, BASE)
-    spilled = jnp.max(spilled) > 0
-
-    def late():
-        rows = [
-            send(pack_late(wide_count, table, core_at, own, mate))
-            for own, mate in ((own_a, mate_a), (own_b, mate_b))
-        ]
-        return (rows[0], rows[1]) + read_notes(rows[0], EXTRA)[:2]
-
-    def never():
-        rows = [empty((wide_count, EXTRA * ROWS + NOTES, LANES)) for _ in range(2)]
-        count = wide_count // 2 * EXTRA
-        return rows[0], rows[1], jnp.full((count,), -1, jnp.int32), jnp.zeros((count,), jnp.int32)
-
-    more_a, more_b, more_station, more_length = lax.cond(spilled, late, never)
+
+    def late_rows(low, own, mate):
+        return send(pack_rows(low, MOST - low, wide_count, table, core_at, own, mate, jnp.zeros_like(table_notes(packed)))[0])
+
+    def late_a():
+        rows = late_rows(base_a, own_a, mate_a)
+        return (rows,) + read_slots(rows, MOST - base_a)[:2]
+
+    def never_a():
+        count = wide_count // 2 * (MOST - base_a)
+        rows = empty((wide_count, (MOST - base_a) * ROWS + NOTES, LANES))
+        return rows, jnp.full((count,), -1, jnp.int32), jnp.zeros((count,), jnp.int32)
+
+    station, length, spilled = read_slots(got_a, base_a)
+    more_a, more_station, more_length = lax.cond(jnp.max(spilled) > 0, late_a, never_a)
     station = jnp.concatenate([station, more_station])
     length = jnp.concatenate([length, more_length])
     chosen = station[None, :] == jnp.arange(ST_DEV, dtype=jnp.int32)[:, None]
     codes = jnp.arange(station.shape[0], dtype=jnp.int32)
-    source = jnp.max(jnp.where(chosen, codes[None], 0), axis=1)
-    length = jnp.max(jnp.where(chosen, length[None], 0), axis=1)
+    source_a = jnp.sum(jnp.where(chosen, codes[None], 0), axis=1)
+    length = jnp.sum(jnp.where(chosen, length[None], 0), axis=1)
+
+    owner = read_table(got_a, slots, wide_count // 2)
+    source_b, unplaced = second_places(owner, column, base_b)
+    more_b = lax.cond(
+        unplaced,
+        lambda: late_rows(base_b, own_b, mate_b),
+        lambda: empty((wide_count, (MOST - base_b) * ROWS + NOTES, LANES)),
+    )
 
     tables = [jnp.asarray(table) for table in transform_tables()]
     near_pick = own_pick[0, 0].reshape(stops, -1)
-    white_a, home, *payload_a = whiten(0, stops, source, length, by_stop, got_a, more_a, tables, [])
+    white_a, home, *payload_a = whiten(0, stops, source_a, length, by_stop, got_a, more_a, tables, [])
     far_a = [
         lax.ppermute(payload_a[stop - 1][0], "blk", [(i, (i + stop) % stops) for i in range(stops)])
         for stop in range(1, stops)
     ]
-    white_b, payload_b = whiten(1, 1, source, length, by_dest, got_b, more_b, tables, far_a)
+    white_b, payload_b = whiten(1, 1, source_b, length, by_dest, got_b, more_b, tables, far_a)
     far_b = lax.all_to_all(payload_b, "blk", split_axis=0, concat_axis=0, tiled=True)
 
     far_at = (group - steps) % stops

time: 216 us -> 205 us (0.949); the launches traced: 213 us -> 205 us
  starting transfers between devices: 54 us -> 47.9 us
  Pallas kernels: 56.1 us -> 50.7 us
  other arithmetic: 10.8 us -> 15.9 us
  local copies, waits for them, and re-layouts: 13.9 us -> 11.4 us
    ppermute x9 -> x7, waiting for transfers between devices: 4.87 us -> 14.7 us  [across(): lax.ppermute(shard, 'wide', [(i, i ^ bits) for i in range(wide_count)])]
    ppermute x7 -> x3, waiting for transfers between devices: 12.6 us -> 3.72 us  [on_device(): theirs = lax.ppermute(visits, 'blk', [(i, i ^ bit) for i in range(stops)])]
    pallas_call x5 -> x3, Pallas kernels: 24.9 us -> 19.6 us  [the longest x1 8.66 us: pack_planned(): pl.pallas_call(functools.partial(pack_kernel, base), out_shape=jax.ShapeD...]
    reduce_sum x0 -> x5, other arithmetic: none -> 5.32 us  [the longest x1 1.74 us: second_places(): guest = jnp.sum((alike & sent[:, None, :]).astype(jnp.int32), axis=2)]
    ppermute x7 -> x3, starting transfers between devices: 12.4 us -> 8.19 us  [on_device(): theirs = lax.ppermute(visits, 'blk', [(i, i ^ bit) for i in range(stops)])]
    all_to_all x2, starting transfers between devices: 19 us -> 16.1 us  [send(): lax.all_to_all(payload, 'wide', split_axis=0, concat_axis=0, tiled=True)]
    ppermute x7, starting transfers between devices: 6.61 us -> 9.36 us  [on_device(): lax.ppermute(payload_a[stop - 1][0], 'blk', [(i, (i + stop) % stops) for...]
    unnamed x38 -> x33, local copies, waits for them, and re-layouts: 4.54 us -> 2.1 us
  transfers between devices with their start and end apart: 26 -> 20, of which waited for: 14 -> 13; matrix products, arithmetic and copies ran while one was open for 6% -> 6% of each run, Pallas kernels for 13% -> 10%
where the time goes in v1:
time: 205 us
  waiting for transfers between devices  76.2 us (37%)
  Pallas kernels  50.7 us (25%)
  starting transfers between devices  47.9 us (23%)
  other arithmetic  15.9 us (8%)
  local copies, waits for them, and re-layouts  11.4 us (6%)
  between operations  2.54 us (1%)
    ppermute x7, waiting for transfers between devices, on_device(): lax.ppermute(payload_a[stop - 1][0], 'blk', [(i, (i + stop) % stops) for...  30.7 us
    all_to_all x1, waiting for transfers between devices, on_device(): lax.all_to_all(payload_b, 'blk', split_axis=0, concat_axis=0, tiled=True)  26.4 us
    all_to_all x2, starting transfers between devices, send(): lax.all_to_all(payload, 'wide', split_axis=0, concat_axis=0, tiled=True)  16.1 us
    pallas_call x1, Pallas kernels, lagged(): pl.pallas_call(functools.partial(lag_kernel, stops), out_shape=jax.ShapeD...  16 us
    pallas_call x2, Pallas kernels, whiten(): pl.pallas_call(functools.partial(whiten_kernel, part, parts), out_shape=(...  15.2 us
    ppermute x7, waiting for transfers between devices, across(): lax.ppermute(shard, 'wide', [(i, i ^ bits) for i in range(wide_count)])  14.7 us
    ppermute x7, starting transfers between devices, across(): lax.ppermute(shard, 'wide', [(i, i ^ bits) for i in range(wide_count)])  9.64 us
    ppermute x7, starting transfers between devices, on_device(): lax.ppermute(payload_a[stop - 1][0], 'blk', [(i, (i + stop) % stops) for...  9.36 us
  transfers between devices with their start and end apart: 20, of which 13 were waited for; matrix products, arithmetic and copies ran while one was open for 6% of the time, Pallas kernels for 10%

profile of v1, /device:TPU:1, one launch (start us, length us, event | category | flops | bytes accessed | tf_op | source)
XLA Modules:
  0.0 204.8 jit_solution(17044554213391685656)
XLA Ops:
  0.0 4.5 %slice.78 = bf16[72,2,64,128]{3,1,2,0:T(2,128)(2,1)S(1)} slice(bf16[72,4,64,128]{3,1,2,0:T(4,128)(2,1)} %bitcast.72), slice={[0:72], [0:2], [0:64], [0:128]} | slice | bytes 4718592 | tf_op jit(solution)/shard_map/slice | solution.py:646
  4.5 3.3 %collective-permute-start.3 = (bf16[72,128,128]{2,1,0:T(8,128)(2,1)S(1)}, bf16[72,128,128]{2,1,0:T(8,128)(2,1)}, u32[]{:S(2)}, u32[]{:S(2)}) collective-permute-start(bf16[72,128,128]{2,1,0:T(8,128)(2,1)S(1)} %bitcast.69), channel_id=1, source_target_pairs={{0,8},{8,0},{16,24},{24,16},{32,40},{40,32},{48,56},{56,48},{64,72... | collective-permute-start | bytes 7077896 | tf_op jit(solution)/shard_map/ppermute | solution.py:632
  8.0 1.4 collective-permute-start.1
  12.1 6.7 %pack_rows.5 = (bf16[32,272,128]{2,1,0:T(8,128)(2,1)}, s32[1]{0:T(128)}) custom-call(s32[4,72]{1,0:T(4,128)S(1)} %add_select_fusion.1.table, s32[1]{0:T(128)} %bitcast.6.core_ref, bf16[72,128,128]{2,1,0:T(8,128)(2,1)S(1)} %bitcast.70, bf16[72,128,128]{2,1,0:T(8,128)(2,1)} %collective-permute-done.3.mate, s32[16,128]{1,0:T(8,128)} %pad.9.refs_0_), custom_call_target="tpu_custom_call" | custom-call | bytes 4194304 | tf_op jit(solution)/shard_map/pack_rows/pallas_call | solution.py:149
  18.8 8.1 %all-to-all-start.2 = ((bf16[32,272,128]{2,1,0:T(8,128)(2,1)}), bf16[32,272,128]{2,1,0:T(8,128)(2,1)}, u32[]{:S(2)}, u32[]{:S(2)}) async-start(bf16[32,272,128]{2,1,0:T(8,128)(2,1)} %get-tuple-element.54), calls=%async_computation.2 | async-start | bytes 4456448 | tf_op jit(solution)/shard_map/all_to_all | solution.py:649
  27.5 6.0 %broadcast_select_fusion = bf16[72,2,64,128]{3,1,2,0:T(2,128)(2,1)S(1)} fusion(pred[]{:T(512)} %bitcast.12, bf16[72,4,64,128]{3,1,2,0:T(4,128)(2,1)} %bitcast.73), kind=kLoop, calls=%fused_computation.6 | loop fusion | flops 1179648 | bytes 4718593 | tf_op jit(solution)/shard_map/jit(_where)/select_n | solution.py:656
  35.3 1.8 collective-permute-done.4
  37.1 2.5 %collective-permute-start.5 = (s32[2,8,8]{2,1,0:T(8,128)S(1)}, s32[2,8,8]{2,1,0:T(8,128)S(1)}, u32[]{:S(2)}, u32[]{:S(2)}) collective-permute-start(s32[2,8,8]{2,1,0:T(8,128)S(1)} %pad_add_fusion.3), channel_id=1, source_target_pairs={{0,2},{1,3},{2,0},{3,1},{4,6},{5,7},{6,4},{7,5},{8,10},{9,11},{10,... | collective-permute-start | bytes 1544 | tf_op jit(solution)/shard_map/ppermute | solution.py:663
  39.6 2.0 collective-permute-done.5
  41.6 4.5 %collective-permute-start.6 = (s32[4,8,8]{2,1,0:T(8,128)S(1)}, s32[4,8,8]{2,1,0:T(8,128)S(1)}, u32[]{:S(2)}, u32[]{:S(2)}) collective-permute-start(s32[4,8,8]{2,1,0:T(8,128)S(1)} %pad_add_fusion.1), channel_id=1, source_target_pairs={{0,4},{1,5},{2,6},{3,7},{4,0},{5,1},{6,2},{7,3},{8,12},{9,13},{10,... | collective-permute-start | bytes 3080 | tf_op jit(solution)/shard_map/ppermute | solution.py:663
  46.1 4.2 %spill.1 = (bf16[12,64,128]{2,1,0:T(8,128)(2,1)}, bf16[12,64,128]{2,1,0:T(8,128)(2,1)}, s32[2,72]{1,0:T(2,128)}, s32[32]{0:T(128)}) custom-call(s32[4,72]{1,0:T(4,128)S(1)} %add_select_fusion.1.table, s32[1]{0:T(128)} %bitcast.6.core_ref, bf16[72,128,128]{2,1,0:T(8,128)(2,1)S(1)} %bitcast.66), custom_call_target="tpu_custom_call" | custom-call | bytes 1048576 | tf_op jit(solution)/shard_map/spill/pallas_call | solution.py:208
  51.1 2.9 %collective-permute-start.16 = (bf16[12,64,128]{2,1,0:T(8,128)(2,1)}, bf16[12,64,128]{2,1,0:T(8,128)(2,1)S(1)}, u32[]{:S(2)}, u32[]{:S(2)}) collective-permute-start(bf16[12,64,128]{2,1,0:T(8,128)(2,1)} %get-tuple-element.71), channel_id=1, source_target_pairs={{0,136},{8,128},{16,152},{24,144},{32,168},{40,160},{48,184},{56,1... | collective-permute-start | bytes 589832 | tf_op jit(solution)/shard_map/ppermute | solution.py:632
  55.8 2.3 %collective-permute-done.15.same = bf16[12,64,128]{2,1,0:T(8,128)(2,1)S(1)} collective-permute-done((bf16[12,64,128]{2,1,0:T(8,128)(2,1)}, bf16[12,64,128]{2,1,0:T(8,128)(2,1)S(1)}, u32[]{:S(2)}, u32[]{:S(2)}) %collective-permute-start.15) | collective-permute-done | bytes 196640 | tf_op jit(solution)/shard_map/ppermute | solution.py:632
  58.0 11.1 %collective-permute-done.16.other = bf16[12,64,128]{2,1,0:T(8,128)(2,1)S(1)} collective-permute-done((bf16[12,64,128]{2,1,0:T(8,128)(2,1)}, bf16[12,64,128]{2,1,0:T(8,128)(2,1)S(1)}, u32[]{:S(2)}, u32[]{:S(2)}) %collective-permute-start.16) | collective-permute-done | bytes 196640 | tf_op jit(solution)/shard_map/ppermute | solution.py:632
  69.9 8.7 %pack_planned.1 = bf16[32,192,128]{2,1,0:T(8,128)(2,1)} custom-call(s32[4,72]{1,0:T(4,128)S(1)} %add_select_fusion.1.table, s32[2,72]{1,0:T(2,128)} %get-tuple-element.68.plan, s32[32]{0:T(128)} %get-tuple-element.69.held, s32[1]{0:T(128)} %bitcast.6.core_ref, bf16[72,128,128]{2,1,0:T(8,128)(2,1)S(1)} %bitcast.67, ...), custom_call_target="tpu_custom_call" | custom-call | bytes 3145728 | tf_op jit(solution)/shard_map/pack_planned/pallas_call | solution.py:285
  79.2 1.2 convert_reduce_fusion.4
  82.9 1.1 convert_reduce_fusion.3
  84.7 1.7 convert_reduce_fusion
  88.2 8.0 %all-to-all-start.3 = ((bf16[32,192,128]{2,1,0:T(8,128)(2,1)}), bf16[32,192,128]{2,1,0:T(8,128)(2,1)}, u32[]{:S(2)}, u32[]{:S(2)}) async-start(bf16[32,192,128]{2,1,0:T(8,128)(2,1)} %pack_planned.1), calls=%async_computation.3 | async-start | bytes 3145728 | tf_op jit(solution)/shard_map/all_to_all | solution.py:649
  97.4 7.6 %whiten.2 = (bf16[24,2,64,128]{3,2,1,0:T(8,128)(2,1)}, bf16[1,8,2,64,128]{4,3,2,1,0:T(8,128)(2,1)}, bf16[1,8,2,64,128]{4,3,2,1,0:T(8,128)(2,1)}, bf16[1,8,2,64,1...) custom-call(s32[24]{0:T(128)} %get-tuple-element.77.source, ...), custom_call_target="tpu_custom_call" | custom-call | flops 629145600 | bytes 4194304 | tf_op jit(solution)/shard_map/whiten/pallas_call | solution.py:448
  105.1 2.7 %collective-permute-start.8 = (bf16[8,2,64,128]{3,2,1,0:T(8,128)(2,1)}, bf16[8,2,64,128]{3,2,1,0:T(8,128)(2,1)S(1)}, u32[]{:S(2)}, u32[]{:S(2)}) collective-permute-start(bf16[8,2,64,128]{3,2,1,0:T(8,128)(2,1)} %bitcast.98), channel_id=1, source_target_pairs={{0,2},{1,3},{2,4},{3,5},{4,6},{5,7},{6,0},{7,1},{8,10},{9,11},{10,... | collective-permute-start | bytes 786440 | tf_op jit(solution)/shard_map/ppermute | solution.py:705
  107.8 2.1 %collective-permute-start.9 = (bf16[8,2,64,128]{3,2,1,0:T(8,128)(2,1)}, bf16[8,2,64,128]{3,2,1,0:T(8,128)(2,1)S(1)}, u32[]{:S(2)}, u32[]{:S(2)}) collective-permute-start(bf16[8,2,64,128]{3,2,1,0:T(8,128)(2,1)} %bitcast.97), channel_id=1, source_target_pairs={{0,3},{1,4},{2,5},{3,6},{4,7},{5,0},{6,1},{7,2},{8,11},{9,12},{10,... | collective-permute-start | bytes 786440 | tf_op jit(solution)/shard_map/ppermute | solution.py:705
  110.9 3.2 %collective-permute-start.11 = (bf16[8,2,64,128]{3,2,1,0:T(8,128)(2,1)}, bf16[8,2,64,128]{3,2,1,0:T(8,128)(2,1)S(1)}, u32[]{:S(2)}, u32[]{:S(2)}) collective-permute-start(bf16[8,2,64,128]{3,2,1,0:T(8,128)(2,1)} %bitcast.95), channel_id=1, source_target_pairs={{0,5},{1,6},{2,7},{3,0},{4,1},{5,2},{6,3},{7,4},{8,13},{9,14},{10,... | collective-permute-start | bytes 786440 | tf_op jit(solution)/shard_map/ppermute | solution.py:705
  114.1 19.1 %collective-permute-done.7.refs_0_ = bf16[8,2,64,128]{3,2,1,0:T(8,128)(2,1)S(1)} collective-permute-done((bf16[8,2,64,128]{3,2,1,0:T(8,128)(2,1)}, bf16[8,2,64,128]{3,2,1,0:T(8,128)(2,1)S(1)}, u32[]{:S(2)}, u32[]{:S(2)}) %collective-permute-start.7) | collective-permute-done | bytes 262176 | tf_op jit(solution)/shard_map/ppermute | solution.py:705
  134.8 1.2 collective-permute-done.9.refs_2_
  135.9 8.6 %collective-permute-done.10.refs_3_ = bf16[8,2,64,128]{3,2,1,0:T(8,128)(2,1)S(1)} collective-permute-done((bf16[8,2,64,128]{3,2,1,0:T(8,128)(2,1)}, bf16[8,2,64,128]{3,2,1,0:T(8,128)(2,1)S(1)}, u32[]{:S(2)}, u32[]{:S(2)}) %collective-permute-start.10) | collective-permute-done | bytes 262176 | tf_op jit(solution)/shard_map/ppermute | solution.py:705
  144.6 1.8 collective-permute-done.13.refs_6_
  146.4 7.6 %whiten.3 = (bf16[24,2,64,128]{3,2,1,0:T(8,128)(2,1)}, bf16[8,8,2,64,128]{4,3,2,1,0:T(8,128)(2,1)}) custom-call(s32[24]{0:T(128)} %select_reduce_fusion.source, s32[24]{0:T(128)} %get-tuple-element.76.length, s32[8,8]{1,0:T(8,128)} %copy-done.8, bf16[32,192,128]{2,1,0:T(8,128)(2,1)} %all-to-all-done.3.got, ...), custom_call_target="tpu_custom_call" | custom-call | flops 629145600 | bytes 4194304 | tf_op jit(solution)/shard_map/whiten/pallas_call | solution.py:448
  154.1 4.7 %all-to-all-start.4 = ((bf16[8,8,2,64,128]{4,3,2,1,0:T(8,128)(2,1)}), bf16[8,8,2,64,128]{4,3,2,1,0:T(8,128)(2,1)S(1)}, u32[]{:S(2)}, u32[]{:S(2)}) async-start(bf16[8,8,2,64,128]{4,3,2,1,0:T(8,128)(2,1)} %get-tuple-element.73), calls=%async_computation.4 | async-start | bytes 4194304 | tf_op jit(solution)/shard_map/all_to_all | solution.py:709
  160.9 26.4 %all-to-all-done.4.refs_8_ = bf16[8,8,2,64,128]{4,3,2,1,0:T(8,128)(2,1)S(1)} async-done(((bf16[8,8,2,64,128]{4,3,2,1,0:T(8,128)(2,1)}), bf16[8,8,2,64,128]{4,3,2,1,0:T(8,128)(2,1)S(1)}, u32[]{:S(2)}, u32[]{:S(2)}) %all-to-all-start.4) | async-done | bytes 2097184 | tf_op jit(solution)/shard_map/all_to_all | solution.py:709
  187.3 1.3 copy-done.1
  188.6 16.0 %lagged.1 = f32[64,4,1024]{2,1,0:T(4,128)} custom-call(s32[8,8]{1,0:T(8,128)} %copy.75.near_pick, s32[8]{0:T(128)} %and_select_fusion.4.far_at, bf16[24,2,64,128]{3,2,1,0:T(8,128)(2,1)} %get-tuple-element.59.white_a, bf16[8,2,64,128]{3,2,1,0:T(8,128)(2,1)} %bitcast.74, bf16[8,2,64,128]{3,2,1,0:T(8,128)(2,1)} %copy-done.2, bf16[8,2,64,128]{3,2,1,0:T(8,128)(2,1)} %copy-done.3, ...), custom_call_target="tpu_custom_call" | custom-call | flops 2147483648 | bytes 16777216 | tf_op jit(solution)/shard_map/lagged/pallas_call | solution.py:589
  (118 shorter events, 18.0 us)
Async XLA Ops:
  0.0 7.8 %copy-start.14 = (s32[1,72]{1,0:T(1,128)S(1)}, s32[1,72]{1,0:T(1,128)}, u32[]{:S(2)}) copy-start(s32[1,72]{1,0:T(1,128)} %param.16) | copy-start | bytes 868
  0.0 7.8 %copy-start.15 = (s32[1,72]{1,0:T(1,128)S(1)}, s32[1,72]{1,0:T(1,128)}, u32[]{:S(2)}) copy-start(s32[1,72]{1,0:T(1,128)} %param.17) | copy-start | bytes 868
  4.5 14.3 %copy-start = (bf16[72,2,64,128]{3,1,2,0:T(2,128)(2,1)}, bf16[72,2,64,128]{3,1,2,0:T(2,128)(2,1)S(1)}, u32[]{:S(2)}) copy-start(bf16[72,2,64,128]{3,1,2,0:T(2,128)(2,1)S(1)} %slice.78) | copy-start | bytes 7077892
  4.5 7.6 %collective-permute-start.3 = (bf16[72,128,128]{2,1,0:T(8,128)(2,1)S(1)}, bf16[72,128,128]{2,1,0:T(8,128)(2,1)}, u32[]{:S(2)}, u32[]{:S(2)}) collective-permute-start(bf16[72,128,128]{2,1,0:T(8,128)(2,1)S(1)} %bitcast.69), channel_id=1, source_target_pairs={{0,8},{8,0},{16,24},{24,16},{32,40},{40,32},{48,56},{56,48},{64,72... | collective-permute-start | bytes 7077896 | tf_op jit(solution)/shard_map/ppermute | solution.py:632
  7.9 3.1 %collective-permute-start.2 = (s32[72]{0:T(128)S(1)}, s32[72]{0:T(128)S(1)}, u32[]{:S(2)}, u32[]{:S(2)}) collective-permute-start(s32[72]{0:T(128)S(1)} %bitcast.85), channel_id=1, source_target_pairs={{0,136},{8,128},{16,152},{24,144},{32,168},{40,160},{48,184},{56,1... | collective-permute-start | bytes 872 | tf_op jit(solution)/shard_map/ppermute | solution.py:632
  8.0 3.0 %collective-permute-start.1 = (s32[72]{0:T(128)S(1)}, s32[72]{0:T(128)S(1)}, u32[]{:S(2)}, u32[]{:S(2)}) collective-permute-start(s32[72]{0:T(128)S(1)} %bitcast.86), channel_id=1, source_target_pairs={{0,128},{8,136},{16,144},{24,152},{32,160},{40,168},{48,176},{56,1... | collective-permute-start | bytes 872 | tf_op jit(solution)/shard_map/ppermute | solution.py:632
  9.3 2.7 %collective-permute-start = (s32[72]{0:T(128)S(1)}, s32[72]{0:T(128)S(1)}, u32[]{:S(2)}, u32[]{:S(2)}) collective-permute-start(s32[72]{0:T(128)S(1)} %bitcast.87), channel_id=1, source_target_pairs={{0,8},{8,0},{16,24},{24,16},{32,40},{40,32},{48,56},{56,48},{64,72... | collective-permute-start | bytes 872 | tf_op jit(solution)/shard_map/ppermute | solution.py:632
  18.8 60.4 %all-to-all-start.2 = ((bf16[32,272,128]{2,1,0:T(8,128)(2,1)}), bf16[32,272,128]{2,1,0:T(8,128)(2,1)}, u32[]{:S(2)}, u32[]{:S(2)}) async-start(bf16[32,272,128]{2,1,0:T(8,128)(2,1)} %get-tuple-element.54), calls=%async_computation.2 | async-start | bytes 4456448 | tf_op jit(solution)/shard_map/all_to_all | solution.py:649
  27.5 6.6 %copy-start.12 = (s32[1,1,8,2,4]{2,4,3,1,0:T(4,128)S(1)}, s32[1,1,8,2,4]{2,4,3,1,0:T(4,128)}, u32[]{:S(2)}) copy-start(s32[1,1,8,2,4]{2,4,3,1,0:T(4,128)} %param.19) | copy-start | bytes 772
  33.5 22.3 %collective-permute-start.14 = (bf16[72,128,128]{2,1,0:T(8,128)(2,1)S(1)}, bf16[72,128,128]{2,1,0:T(8,128)(2,1)}, u32[]{:S(2)}, u32[]{:S(2)}) collective-permute-start(bf16[72,128,128]{2,1,0:T(8,128)(2,1)S(1)} %bitcast.65), channel_id=1, source_target_pairs={{0,8},{8,0},{16,24},{24,16},{32,40},{40,32},{48,56},{56,48},{64,72... | collective-permute-start | bytes 7077896 | tf_op jit(solution)/shard_map/ppermute | solution.py:632
  34.2 2.9 %collective-permute-start.4 = (s32[1,8,8]{2,1,0:T(8,128)S(1)}, s32[1,8,8]{2,1,0:T(8,128)S(1)}, u32[]{:S(2)}, u32[]{:S(2)}) collective-permute-start(s32[1,8,8]{2,1,0:T(8,128)S(1)} %copy.68), channel_id=1, source_target_pairs={{0,1},{1,0},{2,3},{3,2},{4,5},{5,4},{6,7},{7,6},{8,9},{9,8},{10,11... | collective-permute-start | bytes 776 | tf_op jit(solution)/shard_map/ppermute | solution.py:663
  37.1 4.5 %collective-permute-start.5 = (s32[2,8,8]{2,1,0:T(8,128)S(1)}, s32[2,8,8]{2,1,0:T(8,128)S(1)}, u32[]{:S(2)}, u32[]{:S(2)}) collective-permute-start(s32[2,8,8]{2,1,0:T(8,128)S(1)} %pad_add_fusion.3), channel_id=1, source_target_pairs={{0,2},{1,3},{2,0},{3,1},{4,6},{5,7},{6,4},{7,5},{8,10},{9,11},{10,... | collective-permute-start | bytes 1544 | tf_op jit(solution)/shard_map/ppermute | solution.py:663
  41.6 12.4 %collective-permute-start.6 = (s32[4,8,8]{2,1,0:T(8,128)S(1)}, s32[4,8,8]{2,1,0:T(8,128)S(1)}, u32[]{:S(2)}, u32[]{:S(2)}) collective-permute-start(s32[4,8,8]{2,1,0:T(8,128)S(1)} %pad_add_fusion.1), channel_id=1, source_target_pairs={{0,4},{1,5},{2,6},{3,7},{4,0},{5,1},{6,2},{7,3},{8,12},{9,13},{10,... | collective-permute-start | bytes 3080 | tf_op jit(solution)/shard_map/ppermute | solution.py:663
  50.3 7.7 %collective-permute-start.15 = (bf16[12,64,128]{2,1,0:T(8,128)(2,1)}, bf16[12,64,128]{2,1,0:T(8,128)(2,1)S(1)}, u32[]{:S(2)}, u32[]{:S(2)}) collective-permute-start(bf16[12,64,128]{2,1,0:T(8,128)(2,1)} %get-tuple-element.70), channel_id=1, source_target_pairs={{0,128},{8,136},{16,144},{24,152},{32,160},{40,168},{48,176},{56,1... | collective-permute-start | bytes 589832 | tf_op jit(solution)/shard_map/ppermute | solution.py:632
  51.1 18.0 %collective-permute-start.16 = (bf16[12,64,128]{2,1,0:T(8,128)(2,1)}, bf16[12,64,128]{2,1,0:T(8,128)(2,1)S(1)}, u32[]{:S(2)}, u32[]{:S(2)}) collective-permute-start(bf16[12,64,128]{2,1,0:T(8,128)(2,1)} %get-tuple-element.71), channel_id=1, source_target_pairs={{0,136},{8,128},{16,152},{24,144},{32,168},{40,160},{48,184},{56,1... | collective-permute-start | bytes 589832 | tf_op jit(solution)/shard_map/ppermute | solution.py:632
  54.6 23.9 %copy-start.8 = (s32[8,8]{1,0:T(8,128)}, s32[8,8]{1,0:T(8,128)S(1)}, u32[]{:S(2)}) copy-start(s32[8,8]{1,0:T(8,128)S(1)} %gather_fusion) | copy-start | bytes 772
  58.0 11.1 %copy-start.9 = (bf16[12,64,128]{2,1,0:T(8,128)(2,1)}, bf16[12,64,128]{2,1,0:T(8,128)(2,1)S(1)}, u32[]{:S(2)}) copy-start(bf16[12,64,128]{2,1,0:T(8,128)(2,1)S(1)} %collective-permute-done.15.same) | copy-start | bytes 589828
  88.2 58.2 %all-to-all-start.3 = ((bf16[32,192,128]{2,1,0:T(8,128)(2,1)}), bf16[32,192,128]{2,1,0:T(8,128)(2,1)}, u32[]{:S(2)}, u32[]{:S(2)}) async-start(bf16[32,192,128]{2,1,0:T(8,128)(2,1)} %pack_planned.1), calls=%async_computation.3 | async-start | bytes 3145728 | tf_op jit(solution)/shard_map/all_to_all | solution.py:649
  105.0 28.2 %collective-permute-start.7 = (bf16[8,2,64,128]{3,2,1,0:T(8,128)(2,1)}, bf16[8,2,64,128]{3,2,1,0:T(8,128)(2,1)S(1)}, u32[]{:S(2)}, u32[]{:S(2)}) collective-permute-start(bf16[8,2,64,128]{3,2,1,0:T(8,128)(2,1)} %bitcast.99), channel_id=1, source_target_pairs={{0,1},{1,2},{2,3},{3,4},{4,5},{5,6},{6,7},{7,0},{8,9},{9,10},{10,1... | collective-permute-start | bytes 786440 | tf_op jit(solution)/shard_map/ppermute | solution.py:705
  105.1 28.1 %collective-permute-start.8 = (bf16[8,2,64,128]{3,2,1,0:T(8,128)(2,1)}, bf16[8,2,64,128]{3,2,1,0:T(8,128)(2,1)S(1)}, u32[]{:S(2)}, u32[]{:S(2)}) collective-permute-start(bf16[8,2,64,128]{3,2,1,0:T(8,128)(2,1)} %bitcast.98), channel_id=1, source_target_pairs={{0,2},{1,3},{2,4},{3,5},{4,6},{5,7},{6,0},{7,1},{8,10},{9,11},{10,... | collective-permute-start | bytes 786440 | tf_op jit(solution)/shard_map/ppermute | solution.py:705
  107.8 28.1 %collective-permute-start.9 = (bf16[8,2,64,128]{3,2,1,0:T(8,128)(2,1)}, bf16[8,2,64,128]{3,2,1,0:T(8,128)(2,1)S(1)}, u32[]{:S(2)}, u32[]{:S(2)}) collective-permute-start(bf16[8,2,64,128]{3,2,1,0:T(8,128)(2,1)} %bitcast.97), channel_id=1, source_target_pairs={{0,3},{1,4},{2,5},{3,6},{4,7},{5,0},{6,1},{7,2},{8,11},{9,12},{10,... | collective-permute-start | bytes 786440 | tf_op jit(solution)/shard_map/ppermute | solution.py:705
  110.0 34.6 %collective-permute-start.10 = (bf16[8,2,64,128]{3,2,1,0:T(8,128)(2,1)}, bf16[8,2,64,128]{3,2,1,0:T(8,128)(2,1)S(1)}, u32[]{:S(2)}, u32[]{:S(2)}) collective-permute-start(bf16[8,2,64,128]{3,2,1,0:T(8,128)(2,1)} %bitcast.96), channel_id=1, source_target_pairs={{0,4},{1,5},{2,6},{3,7},{4,0},{5,1},{6,2},{7,3},{8,12},{9,13},{10,... | collective-permute-start | bytes 786440 | tf_op jit(solution)/shard_map/ppermute | solution.py:705
  110.9 33.6 %collective-permute-start.11 = (bf16[8,2,64,128]{3,2,1,0:T(8,128)(2,1)}, bf16[8,2,64,128]{3,2,1,0:T(8,128)(2,1)S(1)}, u32[]{:S(2)}, u32[]{:S(2)}) collective-permute-start(bf16[8,2,64,128]{3,2,1,0:T(8,128)(2,1)} %bitcast.95), channel_id=1, source_target_pairs={{0,5},{1,6},{2,7},{3,0},{4,1},{5,2},{6,3},{7,4},{8,13},{9,14},{10,... | collective-permute-start | bytes 786440 | tf_op jit(solution)/shard_map/ppermute | solution.py:705
  133.2 13.2 %copy-start.2 = (bf16[8,2,64,128]{3,2,1,0:T(8,128)(2,1)}, bf16[8,2,64,128]{3,2,1,0:T(8,128)(2,1)S(1)}, u32[]{:S(2)}) copy-start(bf16[8,2,64,128]{3,2,1,0:T(8,128)(2,1)S(1)} %collective-permute-done.7.refs_0_) | copy-start | bytes 786436
  133.2 11.3 %collective-permute-start.12 = (bf16[8,2,64,128]{3,2,1,0:T(8,128)(2,1)}, bf16[8,2,64,128]{3,2,1,0:T(8,128)(2,1)S(1)}, u32[]{:S(2)}, u32[]{:S(2)}) collective-permute-start(bf16[8,2,64,128]{3,2,1,0:T(8,128)(2,1)} %bitcast.94), channel_id=1, source_target_pairs={{0,6},{1,7},{2,0},{3,1},{4,2},{5,3},{6,4},{7,5},{8,14},{9,15},{10,... | collective-permute-start | bytes 786440 | tf_op jit(solution)/shard_map/ppermute | solution.py:705
  133.2 13.1 %copy-start.3 = (bf16[8,2,64,128]{3,2,1,0:T(8,128)(2,1)}, bf16[8,2,64,128]{3,2,1,0:T(8,128)(2,1)S(1)}, u32[]{:S(2)}) copy-start(bf16[8,2,64,128]{3,2,1,0:T(8,128)(2,1)S(1)} %collective-permute-done.8.refs_1_) | copy-start | bytes 786436
  133.3 13.1 %collective-permute-start.13 = (bf16[8,2,64,128]{3,2,1,0:T(8,128)(2,1)}, bf16[8,2,64,128]{3,2,1,0:T(8,128)(2,1)}, u32[]{:S(2)}, u32[]{:S(2)}) collective-permute-start(bf16[8,2,64,128]{3,2,1,0:T(8,128)(2,1)} %bitcast.93), channel_id=1, source_target_pairs={{0,7},{1,0},{2,1},{3,2},{4,3},{5,4},{6,5},{7,6},{8,15},{9,8},{10,9... | collective-permute-start | bytes 786440 | tf_op jit(solution)/shard_map/ppermute | solution.py:705
  135.9 10.4 %copy-start.4 = (bf16[8,2,64,128]{3,2,1,0:T(8,128)(2,1)}, bf16[8,2,64,128]{3,2,1,0:T(8,128)(2,1)S(1)}, u32[]{:S(2)}) copy-start(bf16[8,2,64,128]{3,2,1,0:T(8,128)(2,1)S(1)} %collective-permute-done.9.refs_2_) | copy-start | bytes 786436
  144.6 1.9 copy-start.7
  154.0 4.7 %copy-start.13 = (s32[1,1,8,2,4]{2,4,3,1,0:T(4,128)S(1)}, s32[1,1,8,2,4]{2,4,3,1,0:T(4,128)}, u32[]{:S(2)}) copy-start(s32[1,1,8,2,4]{2,4,3,1,0:T(4,128)} %param.18) | copy-start | bytes 772
  154.1 5.3 %copy-start.11 = (s32[1,1,8,2,4,4]{2,5,4,3,1,0:T(4,128)S(1)}, s32[1,1,8,2,4,4]{2,5,4,3,1,0:T(4,128)}, u32[]{:S(2)}) copy-start(s32[1,1,8,2,4,4]{2,5,4,3,1,0:T(4,128)} %param.20) | copy-start | bytes 3076
  154.1 33.2 %all-to-all-start.4 = ((bf16[8,8,2,64,128]{4,3,2,1,0:T(8,128)(2,1)}), bf16[8,8,2,64,128]{4,3,2,1,0:T(8,128)(2,1)S(1)}, u32[]{:S(2)}, u32[]{:S(2)}) async-start(bf16[8,8,2,64,128]{4,3,2,1,0:T(8,128)(2,1)} %get-tuple-element.73), calls=%async_computation.4 | async-start | bytes 4194304 | tf_op jit(solution)/shard_map/all_to_all | solution.py:709
  (4 other events, 5.8 us)
